TPU v7x, 128 devices: a whole 4x4x4 slice. The times are simulated.
128 devices in a mesh: pipe: 8 (over z_lo, x), tensor: 4 (over z_hi, core), dp: 4 (over y).
Axes of the slice: x: 4, y: 4, z: 4 (z_hi: 2, z_lo: 2; z = z_hi * 2 + z_lo), core: 2. Of those that a mesh axis runs over, the one named last changes fastest.
Arguments:
- encoded: bfloat16 [4, 1024, 4096], P('dp', 'pipe'), may hold values from -6 to 6
- kv_weight: bfloat16 [8, 2, 4096, 2048], P('pipe', None, None, 'tensor'), may hold values from -0.09375 to 0.09375
- queries: bfloat16 [4, 8, 512, 2048], P('dp', 'pipe', None, 'tensor'), may hold values from -70 to 70
- cotangent: bfloat16 [4, 8, 512, 2048], P('dp', 'pipe', None, 'tensor'), may hold values from -6 to 6
Outputs:
- attended: bfloat16 [4, 8, 512, 2048], P('dp', 'pipe', None, 'tensor')
- query_grad: bfloat16 [4, 8, 512, 2048], P('dp', 'pipe', None, 'tensor')
- encoded_grad: bfloat16 [4, 1024, 4096], P('dp', 'pipe')
- weight_grad: bfloat16 [8, 2, 4096, 2048], P('pipe', None, 'dp', 'tensor')
All inputs are finite; a program needn't handle non-finite values.
Results may differ from a plain program's by a relative error of at most 0.03.
The roundings to bfloat16 on the way count: a program that leaves them out, or rounds other values in their place, can miss the bound.
Values may be sent and summed in bfloat16 or wider, within the bound.
No kernel may reach another device: no remote copies, remote signals or barrier semaphores. Data moves between devices by JAX's collectives and lax.ppermute only.
A program may use at most 128 MiB of HBM per device.

v0:
```python
import jax
import jax.numpy as jnp
from jax import lax
from jax.sharding import PartitionSpec as P

HEAD_DIM = 256


def attend(q, keys, values, dout):
    heads = q.shape[1] // HEAD_DIM
    scale = HEAD_DIM ** (-0.5)
    q_heads = q.astype(jnp.float32).reshape(q.shape[0], heads, HEAD_DIM)
    k_heads = keys.astype(jnp.float32).reshape(keys.shape[0], heads, HEAD_DIM)
    v_heads = values.astype(jnp.float32).reshape(values.shape[0], heads, HEAD_DIM)
    g_heads = dout.astype(jnp.float32).reshape(dout.shape[0], heads, HEAD_DIM)
    scores = jnp.einsum("qhd,khd->hqk", q_heads, k_heads) * scale
    top = jnp.max(scores, axis=-1, keepdims=True)
    expd = jnp.exp(scores - top)
    probs = expd / jnp.sum(expd, axis=-1, keepdims=True)
    probs_low = lax.optimization_barrier(probs.astype(jnp.bfloat16)).astype(jnp.float32)
    attended = jnp.einsum("hqk,khd->qhd", probs_low, v_heads).reshape(q.shape).astype(jnp.bfloat16)
    dprobs = jnp.einsum("qhd,khd->hqk", g_heads, v_heads)
    att_heads = attended.astype(jnp.float32).reshape(q.shape[0], heads, HEAD_DIM)
    delta = jnp.einsum("qhd,qhd->hq", g_heads, att_heads)
    dscores = probs * (dprobs - delta[:, :, None])
    ds_low = lax.optimization_barrier(dscores.astype(jnp.bfloat16)).astype(jnp.float32)
    query_grad = (
        (scale * jnp.einsum("hqk,khd->qhd", ds_low, k_heads)).reshape(q.shape).astype(jnp.bfloat16)
    )
    key_grad = (
        (scale * jnp.einsum("hqk,qhd->khd", ds_low, q_heads))
        .reshape(keys.shape)
        .astype(jnp.bfloat16)
    )
    value_grad = (
        jnp.einsum("hqk,qhd->khd", probs_low, g_heads).reshape(values.shape).astype(jnp.bfloat16)
    )
    return (attended, query_grad, key_grad, value_grad)


def on_device(encoded, kv_weight, queries, cotangent):
    w_key = kv_weight[0, 0]
    w_value = kv_weight[0, 1]
    q_rows = queries[0, 0]
    g_rows = cotangent[0, 0]
    tdims = (((0,), (0,)), ((), ()))
    whole = lax.all_gather(encoded, "pipe", axis=1, tiled=True)[0]
    keys = jnp.dot(whole, w_key, preferred_element_type=jnp.float32).astype(jnp.bfloat16)
    values = jnp.dot(whole, w_value, preferred_element_type=jnp.float32).astype(jnp.bfloat16)
    attended, query_grad, key_grad, value_grad = attend(q_rows, keys, values, g_rows)
    grad_k = lax.dot_general(whole, key_grad, tdims, preferred_element_type=jnp.float32)
    grad_v = lax.dot_general(whole, value_grad, tdims, preferred_element_type=jnp.float32)
    grad_w = jnp.stack([grad_k, grad_v], 0)
    grad_share = lax.psum_scatter(grad_w, "dp", scatter_dimension=1, tiled=True).astype(
        jnp.bfloat16
    )
    cdims = (((1,), (1,)), ((), ()))
    first = lax.dot_general(key_grad, w_key, cdims, preferred_element_type=jnp.float32)
    partial_rows = lax.psum_scatter(
        first + lax.dot_general(value_grad, w_value, cdims, preferred_element_type=jnp.float32),
        "pipe",
        scatter_dimension=0,
        tiled=True,
    )
    summed = lax.psum(partial_rows, "tensor")
    enc_grad = summed.astype(jnp.bfloat16)
    return (attended[None, None], query_grad[None, None], enc_grad[None], grad_share[None])


def solution(mesh):
    return jax.shard_map(
        on_device,
        mesh=mesh,
        in_specs=(
            P("dp", "pipe", None),
            P("pipe", None, None, "tensor"),
            P("dp", "pipe", None, "tensor"),
            P("dp", "pipe", None, "tensor"),
        ),
        out_specs=(
            P("dp", "pipe", None, "tensor"),
            P("dp", "pipe", None, "tensor"),
            P("dp", "pipe", None),
            P("pipe", None, "dp", "tensor"),
        ),
        check_vma=False,
    )
```

profile of v0, /device:TPU:0, one launch (start us, length us, event | category | flops | bytes accessed | tf_op | source)
XLA Modules:
  0.0 529.0 jit_solution(12949029128466617072)
XLA Ops:
  7.2 0.0 all-gather.2.cloned.1.call-start
  7.2 0.7 all-gather.2.cloned.1.call-update
  7.9 0.0 reduce-scatter.5.cloned.1.call-start
  7.9 1.2 reshape.59
  9.1 0.7 copy.17
  9.9 0.0 copy-start
  9.9 1.4 copy.34
  11.3 0.0 copy-start.2
  11.3 92.7 %all-gather.2.cloned.1.call-done = bf16[1,1024,4096]{2,1,0:T(8,128)(2,1)} async-done(((bf16[1,128,4096]{2,1,0:T(8,128)(2,1)}), bf16[1,1024,4096]{2,1,0:T(8,128)(2,1)}) %all-gather.2.cloned.1.call-update) | async-done | bytes 8388624 | tf_op jit(solution)/shard_map/all_gather | solution.py:47
  104.1 9.1 %fusion.37 = bf16[1024,512]{0,1:T(8,128)(2,1)S(1)} fusion(bf16[1,2,4096,512]{3,2,1,0:T(8,128)(2,1)} %param.5, bf16[1,1024,4096]{2,1,0:T(8,128)(2,1)} %all-gather.2.cloned.1.call-done), kind=kOutput, calls=%fused_computation.36 | convolution fusion | flops 4295491584 | bytes 13631488 | tf_op jit(solution)/shard_map/dot_general | solution.py:48
  113.2 0.0 copy-start.4
  113.2 0.0 copy-done.2
  113.2 3.5 fusion.46
  116.7 2.8 fusion.31
  119.5 0.0 copy-done
  119.5 0.0 copy-done.4
  119.5 0.8 convolution_convert_fusion
  120.2 9.1 %fusion.32 = bf16[1024,512]{0,1:T(8,128)(2,1)S(1)} fusion(bf16[1,2,4096,512]{3,2,1,0:T(8,128)(2,1)} %param.5, bf16[1,1024,4096]{2,1,0:T(8,128)(2,1)} %all-gather.2.cloned.1.call-done), kind=kOutput, calls=%fused_computation.35 | convolution fusion | flops 4295491584 | bytes 13631488 | tf_op jit(solution)/shard_map/dot_general | solution.py:49
  129.3 0.0 copy-start.1
  129.4 1.7 bitcast_convert_fusion
  131.1 0.0 copy-done.1
  131.1 1.5 copy.29
  132.6 0.7 multiply_reduce_fusion
  133.3 0.1 copy.30
  133.4 3.6 fusion.15
  137.0 0.0 copy-done.3
  137.0 0.0 copy-start.6
  137.0 0.0 slice-start
  137.0 0.8 multiply_convert_fusion
  137.8 0.5 copy-done.6
  138.3 7.6 %fusion.9 = f32[1,4096,512]{1,2,0:T(8,128)S(1)} fusion(bf16[1024,512]{0,1:T(8,128)(2,1)S(1)} %bitcast.112, bf16[1,1024,4096]{2,1,0:T(8,128)(2,1)} %all-gather.2.cloned.1.call-done), kind=kOutput, calls=%fused_computation.11 | convolution fusion | flops 4294967296 | bytes 17825792 | tf_op jit(solution)/shard_map/dot_general | solution.py:51
  145.9 0.0 slice-done
  146.0 4.6 fusion.12
  150.6 6.0 %pad_maximum_fusion = f32[2,4096,512]{1,2,0:T(8,128)} fusion(f32[1,4096,512]{1,2,0:T(8,128)S(1)} %fusion.12, f32[1,4096,512]{1,2,0:T(8,128)S(1)} %fusion.9), kind=kLoop, calls=%fused_computation.1 | loop fusion | flops 4194304 | bytes 33554432 | tf_op jit(solution)/shard_map/stack | solution.py:53
  156.6 0.0 reduce-scatter.5.cloned.1.call-update
  156.6 0.0 reduce-scatter.3.cloned.1.call-start
  156.6 10.9 %fusion.18 = f32[1024,4096]{1,0:T(8,128)} fusion(bf16[1024,512]{0,1:T(8,128)(2,1)S(1)} %bitcast.113, bf16[1,2,4096,512]{3,2,1,0:T(8,128)(2,1)} %param.5), kind=kOutput, calls=%fused_computation.19 | convolution fusion | flops 4294967296 | bytes 22020096 | tf_op jit(solution)/shard_map/dot_general | solution.py:58
  167.6 12.8 %convolution_add_fusion = f32[1024,4096]{1,0:T(8,128)} fusion(f32[1024,4096]{1,0:T(8,128)} %fusion.18, bf16[1024,512]{0,1:T(8,128)(2,1)S(1)} %bitcast.100, bf16[1,2,4096,512]{3,2,1,0:T(8,128)(2,1)} %param.5), kind=kOutput, calls=%fused_computation.10 | convolution fusion | flops 4299161600 | bytes 38797312 | tf_op jit(solution)/shard_map/dot_general | solution.py:60
  180.4 0.0 reduce-scatter.3.cloned.1.call-update
  180.4 1.2 copy-done.5
  181.6 2.3 fusion.42
  184.0 1.0 copy.19
  185.0 1.0 copy.18
  186.0 117.4 %reduce-scatter.5.cloned.1.call-done = f32[2,1024,512]{1,2,0:T(8,128)} async-done(((f32[2,4096,512]{1,2,0:T(8,128)}), f32[2,1024,512]{1,2,0:T(8,128)}) %reduce-scatter.5.cloned.1.call-update) | async-done | bytes 4194320 | tf_op jit(solution)/shard_map/reduce_scatter | solution.py:54
  303.4 2.5 convert_bitcast_fusion
  305.9 2.6 copy.20
  308.5 168.6 %reduce-scatter.3.cloned.1.call-done = f32[128,4096]{1,0:T(8,128)} async-done(((f32[1024,4096]{1,0:T(8,128)}), f32[128,4096]{1,0:T(8,128)}) %reduce-scatter.3.cloned.1.call-update) | async-done | bytes 2097168 | tf_op jit(solution)/shard_map/reduce_scatter | solution.py:59
  477.1 45.4 %all-reduce.1 = bf16[128,4096]{1,0:T(8,128)(2,1)} all-reduce(f32[128,4096]{1,0:T(8,128)} %reduce-scatter.3.cloned.1.call-done), channel_id=1, replica_groups=mesh['pipe'=8,'tensor'=4,'dp'=4] {'tensor'}, use_global_device_ids=true, to_apply=%region_3.0 | all-reduce | flops 524288 | bytes 3145728 | tf_op jit(solution)/shard_map/psum | solution.py:65
  (5 shorter events, 0.0 us)
Async XLA Ops:
  7.2 96.9 %all-gather.2.cloned.1.call-start = ((), (), s32[]{:S(2)}) async-start(), calls=%async_computation.2 | async-start | bytes 9437184 | tf_op jit(solution)/shard_map/all_gather | solution.py:47
  7.9 295.5 %reduce-scatter.5.cloned.1.call-start = ((), (), s32[]{:S(2)}) async-start(), calls=%async_computation.4 | async-start | bytes 20971520 | tf_op jit(solution)/shard_map/reduce_scatter | solution.py:54
  9.9 109.6 %copy-start = (bf16[512,2,256]{0,2,1:T(8,128)(2,1)}, bf16[512,2,256]{0,2,1:T(8,128)(2,1)S(1)}, u32[]{:S(2)}) copy-start(bf16[512,2,256]{0,2,1:T(8,128)(2,1)S(1)} %copy.17) | copy-start | bytes 1572868
  11.3 101.9 %copy-start.2 = (bf16[1,1,512,512]{2,3,1,0:T(8,128)(2,1)}, bf16[1,1,512,512]{2,3,1,0:T(8,128)(2,1)S(1)}, u32[]{:S(2)}) copy-start(bf16[1,1,512,512]{2,3,1,0:T(8,128)(2,1)S(1)} %copy.34) | copy-start | bytes 1572868
  113.2 6.3 %copy-start.4 = (bf16[1024,512]{0,1:T(8,128)(2,1)}, bf16[1024,512]{0,1:T(8,128)(2,1)S(1)}, u32[]{:S(2)}) copy-start(bf16[1024,512]{0,1:T(8,128)(2,1)S(1)} %fusion.37) | copy-start | bytes 3145732
  129.3 1.7 copy-start.1
  133.4 3.6 copy-start.3
  137.0 1.3 copy-start.6
  137.0 8.9 %slice-start = ((s8[8388608]{0:T(1024)(128)(4,1)}), s8[4194304]{0:T(1024)(128)(4,1)S(1)}, s32[]{:S(2)}) async-start(s8[8388608]{0:T(1024)(128)(4,1)} %bitcast.108), calls=%async_computation.5 | async-start | bytes 8388608
  138.3 7.6 %slice-start.1 = ((s8[8388608]{0:T(1024)(128)(4,1)}), s8[4194304]{0:T(1024)(128)(4,1)S(1)}, s32[]{:S(2)}) async-start(s8[8388608]{0:T(1024)(128)(4,1)} %bitcast.108), calls=%async_computation.6 | async-start | bytes 8388608
  156.6 320.5 %reduce-scatter.3.cloned.1.call-start = ((), (), s32[]{:S(2)}) async-start(), calls=%async_computation.3 | async-start | bytes 18874368 | tf_op jit(solution)/shard_map/reduce_scatter | solution.py:59
  180.4 1.2 copy-start.5
Sparse Core Ops, SparseCore 0:
  9.6 94.4 all-gather.1
  156.7 146.6 reduce-scatter.4
  306.0 171.0 reduce-scatter.2
where the time goes:
time: 531 us; the launch traced here: 529 us
  waiting for transfers between devices  380 us (72%)
  matrix products  66.7 us (13%)
  blocking collectives  45.4 us (9%)
  between operations  14 us (3%)
  other arithmetic  12 us (2%)
  local copies, waits for them, and re-layouts  11.3 us (2%)
    reduce_scatter x1, waiting for transfers between devices, on_device(): lax.psum_scatter(first + lax.dot_general(value_grad, w_value, cdims, pref...  169 us
    reduce_scatter x1, waiting for transfers between devices, on_device(): lax.psum_scatter(grad_w, 'dp', scatter_dimension=1, tiled=True)  117 us
    all_gather x1, waiting for transfers between devices, on_device(): whole = lax.all_gather(encoded, 'pipe', axis=1, tiled=True)[0]  92.7 us
    psum x1, blocking collectives, on_device(): summed = lax.psum(partial_rows, 'tensor')  45.4 us
    dot_general x1, matrix products, on_device(): lax.dot_general(value_grad, w_value, cdims, preferred_element_type=jnp.fl...  12.8 us
    dot_general x1, matrix products, on_device(): lax.dot_general(key_grad, w_key, cdims, preferred_element_type=jnp.float32)  10.9 us
  transfers between devices with their start and end apart: 3, of which 3 were waited for; matrix products, arithmetic and copies ran while one was open for 7% of the time, Pallas kernels for 0%

commit v1 on v0

v1 whole, which is shorter than its diff:
```python
import functools

import jax
import jax.numpy as jnp
from jax import lax
from jax.experimental import pallas as pl
from jax.experimental.pallas import tpu as pltpu
from jax.sharding import PartitionSpec as P

HEAD_DIM = 256
ALL = ("pipe", "tensor", "dp")
F32, BF16 = jnp.float32, jnp.bfloat16
NT = (((1,), (1,)), ((), ()))
TN = (((0,), (0,)), ((), ()))
VMEM_BYTES = 48 * 1024 * 1024


def params():
    return pltpu.CompilerParams(vmem_limit_bytes=VMEM_BYTES)


def cost(flops, nbytes):
    return pl.CostEstimate(flops=flops, bytes_accessed=nbytes, transcendentals=0)


def pairs(move):
    def index(x, y, z, core):
        pipe = (z % 2) * 4 + x
        tensor = (z // 2) * 2 + core
        return (pipe * 4 + tensor) * 4 + y

    found = []
    for x in range(4):
        for y in range(4):
            for z in range(4):
                for core in range(2):
                    to_x, to_y, to_z, to_core = move(x, y, z, core)
                    found.append((index(x, y, z, core), index(to_x, to_y, to_z % 4, to_core)))
    return found


def partner(place, core, which):
    return place ^ 1 if core == which else 3 - place


X_FIRST = pairs(lambda x, y, z, core: (partner(x, core, 0), y, z, core))
X_SECOND = pairs(lambda x, y, z, core: (partner(x, core, 1), y, z, core))
Y_FIRST = pairs(lambda x, y, z, core: (x, partner(y, core, 0), z, core))
Y_SECOND = pairs(lambda x, y, z, core: (x, partner(y, core, 1), z, core))
ALONG_Z = pairs(lambda x, y, z, core: (x, y, z + 1 - 2 * core, core))
BACK_Z = pairs(lambda x, y, z, core: (x, y, z - 1 + 2 * core, core))
ACROSS_Z = pairs(lambda x, y, z, core: (x, y, z + 2, core))
SWAP = pairs(lambda x, y, z, core: (x, y, z, 1 - core))


def send(array, route):
    return lax.ppermute(array, ALL, route)


def project_body(a, b, c, d, w, keys, values, acc):
    x = jnp.concatenate([a[...], b[...], c[...], d[...]], 0)
    step = pl.program_id(0)
    width = keys.shape[1]
    for part in range(2):
        cols = slice(part * width, (part + 1) * width)
        dot = jnp.dot(x, w[0, part], preferred_element_type=F32)

        @pl.when(step == 0)
        def _():
            acc[:, cols] = dot

        @pl.when(step > 0)
        def _():
            acc[:, cols] += dot

    @pl.when(step == pl.num_programs(0) - 1)
    def _():
        keys[...] = acc[:, :width].astype(BF16)
        values[...] = acc[:, width:].astype(BF16)


def project(pieces, kv_weight):
    _, _, depth, width = kv_weight.shape
    rows = 4 * pieces[0].shape[0]
    tile = depth // 4
    shape = jax.ShapeDtypeStruct((rows, width), BF16)
    return pl.pallas_call(
        project_body,
        grid=(4,),
        in_specs=[pl.BlockSpec((rows // 4, tile), lambda i: (0, i))] * 4
        + [pl.BlockSpec((1, 2, tile, width), lambda i: (0, 0, i, 0))],
        out_specs=[pl.BlockSpec((rows, width), lambda i: (0, 0))] * 2,
        out_shape=[shape, shape],
        scratch_shapes=[pltpu.VMEM((rows, 2 * width), F32)],
        compiler_params=params(),
        cost_estimate=cost(4 * rows * depth * width, 4 * depth * width + 2 * rows * depth),
    )(*pieces, kv_weight)


def arrange(groups):
    quarter = groups[0].shape[0] // 4

    def at(group, place):
        return groups[group][place * quarter : (place + 1) * quarter, :]

    order = [(0, 0), (1, 0), (1, 2), (3, 0), (0, 2), (2, 0), (2, 2), (3, 2)]
    return jnp.concatenate(
        [at(g, p) for g, p in order] + [at(g, p + 1) for g, p in order], 0
    )


def attend_body(q, g, k0, k1, k2, k3, v0, v1, v2, v3, att, dq, kg, vg, kgt, vgt, low, dlow):
    scale = HEAD_DIM ** (-0.5)
    k = arrange([k0, k1, k2, k3])
    v = arrange([v0, v1, v2, v3])
    total = q.shape[2]
    chunk = total // 2
    for part in range(2):
        rows = slice(part * chunk, (part + 1) * chunk)
        g_rows = g[0, 0, rows, :]
        scores = lax.dot_general(q[0, 0, rows, :], k, NT, preferred_element_type=F32) * scale
        expd = jnp.exp(scores - jnp.max(scores, axis=-1, keepdims=True))
        probs = expd * (1.0 / jnp.sum(expd, axis=-1, keepdims=True))
        probs_low = probs.astype(BF16)
        low[rows, :] = probs_low
        out = jnp.dot(probs_low, v, preferred_element_type=F32).astype(BF16)
        att[0, 0, rows, :] = out
        dprobs = lax.dot_general(g_rows, v, NT, preferred_element_type=F32)
        delta = jnp.sum(g_rows.astype(F32) * out.astype(F32), axis=-1, keepdims=True)
        ds_low = (probs * (dprobs - delta)).astype(BF16)
        dlow[rows, :] = ds_low
        dq[0, 0, rows, :] = (
            scale * jnp.dot(ds_low, k, preferred_element_type=F32)
        ).astype(BF16)
    value_t = lax.dot_general(g[0, 0], low[...], TN, preferred_element_type=F32)
    vgt[...] = value_t.astype(BF16)
    vg[...] = value_t.T.astype(BF16)
    key_t = scale * lax.dot_general(q[0, 0], dlow[...], TN, preferred_element_type=F32)
    kgt[...] = key_t.astype(BF16)
    kg[...] = key_t.T.astype(BF16)


def attend(queries, cotangent, keys, values):
    _, _, total, width = queries.shape
    rows = keys[0].shape[0]
    span = 4 * rows
    head = pl.BlockSpec((1, 1, total, HEAD_DIM), lambda h: (0, 0, 0, h))
    group = pl.BlockSpec((rows, HEAD_DIM), lambda h: (0, h))
    tall = pl.BlockSpec((span, HEAD_DIM), lambda h: (0, h))
    flat = pl.BlockSpec((HEAD_DIM, span), lambda h: (h, 0))
    same = jax.ShapeDtypeStruct(queries.shape, BF16)
    tall_shape = jax.ShapeDtypeStruct((span, width), BF16)
    flat_shape = jax.ShapeDtypeStruct((width, span), BF16)
    return pl.pallas_call(
        attend_body,
        grid=(width // HEAD_DIM,),
        in_specs=[head, head] + [group] * 8,
        out_specs=[head, head, tall, tall, flat, flat],
        out_shape=[same, same, tall_shape, tall_shape, flat_shape, flat_shape],
        scratch_shapes=[pltpu.VMEM((total, span), BF16)] * 2,
        compiler_params=params(),
        cost_estimate=cost(12 * total * span * width, 16 * span * width),
    )(queries, cotangent, *keys, *values)


def weight_body(count, final, index, grad_t, *refs):
    pieces, refs = refs[:count], refs[count:]
    moved, out = refs[:-1], refs[-1]
    if final:
        moved = [ref for ref in moved if ref.ndim == 2]
    rows = jnp.concatenate([piece[...] for piece in pieces], 0)
    total = jnp.dot(grad_t[...], rows, preferred_element_type=F32)
    for ref in moved:
        total = total + ref[...].astype(F32)
    if final:
        out[0, 0] = total.T.astype(BF16)
    else:
        out[...] = total.astype(BF16)


TILE = 512


def weight_part(index, grad_t, pieces, moved=(), offsets=(), final=None, into=None):
    width, span = grad_t.shape
    steps = index.shape[0]
    depth = pieces[0].shape[1]
    specs = [pl.BlockSpec((width, span), lambda i, index: (0, 0))]
    specs += [pl.BlockSpec((p.shape[0], TILE), lambda i, index: (0, index[i])) for p in pieces]
    for offset in offsets:
        specs.append(
            pl.BlockSpec((width, TILE), functools.partial(lambda o, i, index: (0, o + i), offset))
        )
    operands = [index, grad_t, *pieces, *moved]
    aliases = {}
    if final is None:
        out_spec = pl.BlockSpec((width, TILE), lambda i, index: (0, i))
        out_shape = jax.ShapeDtypeStruct((width, steps * TILE), BF16)
    else:
        out_spec = pl.BlockSpec((1, 1, TILE, width), lambda i, index: (0, final, i, 0))
        out_shape = jax.ShapeDtypeStruct((1, 2, depth // 4, width), BF16)
        if into is not None:
            specs.append(pl.BlockSpec(memory_space=pl.ANY))
            aliases = {len(operands): 0}
            operands.append(into)
    return pl.pallas_call(
        functools.partial(weight_body, len(pieces), final is not None),
        grid_spec=pltpu.PrefetchScalarGridSpec(
            num_scalar_prefetch=1, grid=(steps,), in_specs=specs, out_specs=out_spec
        ),
        out_shape=out_shape,
        input_output_aliases=aliases,
        compiler_params=params(),
        cost_estimate=cost(2 * width * span * TILE * steps, 4 * span * TILE * steps),
    )(*operands)


def encoder_body(kg, vg, w, *refs):
    total = lax.dot_general(kg[...], w[0, 0], NT, preferred_element_type=F32)
    total = total + lax.dot_general(vg[...], w[0, 1], NT, preferred_element_type=F32)
    if len(refs) > 1:
        total = total + refs[0][...].astype(F32)
    refs[-1][...] = total.astype(BF16)


def encoder_part(key_grad, value_grad, kv_weight, block, moved=None):
    span, width = key_grad.shape
    depth = kv_weight.shape[2]
    rows = span // 4
    grad = pl.BlockSpec((rows, width), lambda i: (block, 0))
    tile = pl.BlockSpec((rows, TILE), lambda i: (0, i))
    extra = [] if moved is None else [moved]
    return pl.pallas_call(
        encoder_body,
        grid=(depth // TILE,),
        in_specs=[grad, grad, pl.BlockSpec((1, 2, TILE, width), lambda i: (0, 0, i, 0))]
        + [tile] * len(extra),
        out_specs=tile,
        out_shape=jax.ShapeDtypeStruct((rows, depth), BF16),
        compiler_params=params(),
        cost_estimate=cost(4 * rows * depth * width, 4 * depth * width + 4 * rows * depth),
    )(key_grad, value_grad, kv_weight, *extra)


def tie(array, *others):
    return lax.optimization_barrier((array, *others))[0]


def on_device(encoded, kv_weight, queries, cotangent):
    core = lax.axis_index("tensor") % 2
    y = lax.axis_index("dp")
    block = encoded[0]
    half = block.shape[0] // 2

    h = {"o": lax.dynamic_slice_in_dim(block, core * half, half, 0)}
    h_too = {"o": lax.dynamic_slice_in_dim(block, (1 - core) * half, half, 0)}
    g, g_too = {}, {}
    h["a"] = send(h["o"], X_FIRST)
    g["o"] = send(h["o"], ALONG_Z)
    h["b"] = send(tie(h["o"], h["a"]), X_SECOND)
    g["a"] = send(h["a"], ALONG_Z)
    h["d"] = send(h["a"], X_SECOND)
    g["b"] = send(h["b"], ALONG_Z)
    g["d"] = send(h["d"], ALONG_Z)
    for name in "abd":
        h_too[name] = send(h[name], SWAP)
    for name in "oabd":
        g_too[name] = send(g[name], SWAP)
    groups = [
        (h["o"], h_too["o"], h["a"], h_too["a"]),
        (g["o"], g_too["o"], h["b"], h_too["b"]),
        (g["a"], g_too["a"], h["d"], h_too["d"]),
        (g["b"], g_too["b"], g["d"], g_too["d"]),
    ]
    keys, values = zip(*[project(group, kv_weight) for group in groups])
    order = ["ho", "go", "hb", "gb", "ha", "ga", "hd", "gd"]
    pieces = [{"h": h, "g": g}[name[0]][name[1]] for name in order]
    pieces += [{"h": h_too, "g": g_too}[name[0]][name[1]] for name in order]

    attended, query_grad, key_grad, value_grad, key_grad_t, value_grad_t = attend(
        queries, cotangent, keys, values
    )

    one, other = y ^ 1, 3 - y
    first = jnp.where(core == 0, one, other)
    second = jnp.where(core == 0, other, one)
    across = (y + 2) % 4

    def tiles(*slices):
        return jnp.stack([2 * s + i for s in slices for i in range(2)]).astype(jnp.int32)

    value_out = weight_part(tiles(first, across), value_grad_t, pieces)
    value_in = send(value_out, Y_FIRST)

    key_grad, value_grad = lax.optimization_barrier((key_grad, value_grad, value_out))[:2]
    grads = (key_grad, value_grad, kv_weight)
    moved_send = send(encoder_part(*grads, 3), SWAP)
    moved_keep = send(encoder_part(*grads, 2), SWAP)
    x_out = encoder_part(*grads, 1, moved_send)
    x_in = send(x_out, X_FIRST)
    keep = encoder_part(*grads, 0, moved_keep)

    key_out = weight_part(tiles(first, across), tie(key_grad_t, x_out), pieces)
    key_in = send(key_out, Y_FIRST)

    total = keep.astype(F32) + x_in.astype(F32)
    x_in = send(total[2 * half :].astype(BF16), X_SECOND)
    total = total[: 2 * half] + x_in.astype(F32)
    here = total[:half] + send(total[half:].astype(BF16), BACK_Z).astype(F32)
    here = here.astype(BF16)
    last = (here.astype(F32) + send(here, ACROSS_Z).astype(F32)).astype(BF16)
    last_too = send(last, SWAP)
    enc_grad = jnp.where(
        core == 0, jnp.concatenate([last, last_too], 0), jnp.concatenate([last_too, last], 0)
    )

    value_two = send(
        weight_part(tiles(second), value_grad_t, pieces, [value_in], [2]), Y_SECOND
    )
    key_two = send(weight_part(tiles(second), key_grad_t, pieces, [key_in], [2]), Y_SECOND)
    share = weight_part(tiles(y), value_grad_t, pieces, [value_in, value_two], [0, 0], 1)
    share = weight_part(tiles(y), key_grad_t, pieces, [key_in, key_two], [0, 0], 0, share)
    return (attended, query_grad, enc_grad[None], share)


def solution(mesh):
    return jax.shard_map(
        on_device,
        mesh=mesh,
        in_specs=(
            P("dp", "pipe", None),
            P("pipe", None, None, "tensor"),
            P("dp", "pipe", None, "tensor"),
            P("dp", "pipe", None, "tensor"),
        ),
        out_specs=(
            P("dp", "pipe", None, "tensor"),
            P("dp", "pipe", None, "tensor"),
            P("dp", "pipe", None),
            P("pipe", None, "dp", "tensor"),
        ),
        check_vma=False,
    )
```

time: 531 us -> 232 us (0.44)
  waiting for transfers between devices: 380 us -> 84.3 us
  Pallas kernels: 0 us -> 98.4 us
  matrix products: 66.7 us -> 0 us
  blocking collectives: 45.4 us -> 0 us
  starting transfers between devices: 0.12 us -> 29.9 us
  between operations: 14 us -> 0.92 us
    reduce_scatter x2 -> x0, waiting for transfers between devices: 286 us -> none  [the longest x1 169 us: on_device(): lax.psum_scatter(first + lax.dot_general(value_grad, w_value, cdims, pref...]
    pallas_call x0 -> x15, Pallas kernels: none -> 98.4 us  [the longest x6 34 us: weight_part(): pl.pallas_call(functools.partial(weight_body, len(pieces), final is not N...]
    all_gather x1 -> x0, waiting for transfers between devices: 92.7 us -> none  [on_device(): whole = lax.all_gather(encoded, 'pipe', axis=1, tiled=True)[0]]
    ppermute x0 -> x25, waiting for transfers between devices: none -> 84.3 us  [send(): return lax.ppermute(array, ALL, route)]
    dot_general x11 -> x0, matrix products: 63.3 us -> none  [the longest x1 12.8 us: on_device(): lax.dot_general(value_grad, w_value, cdims, preferred_element_type=jnp.fl...]
    psum x1 -> x0, blocking collectives: 45.4 us -> none  [on_device(): summed = lax.psum(partial_rows, 'tensor')]
    ppermute x0 -> x25, starting transfers between devices: none -> 29.9 us  [send(): return lax.ppermute(array, ALL, route)]
    another operation x1 -> x3, other arithmetic: 6 us -> 0.23 us  [tiles(): jnp.stack([2 * s + i for s in slices for i in range(2)]).astype(jnp.int32)]
  transfers between devices with their start and end apart: 3 -> 25, of which waited for: 3 -> 12; matrix products, arithmetic and copies ran while one was open for 7% -> 2% of each run, Pallas kernels for 0% -> 30%
where the time goes in v1:
time: 232 us; the launch traced here: 231 us
  Pallas kernels  98.4 us (42%)
  waiting for transfers between devices  84.3 us (36%)
  starting transfers between devices  29.9 us (13%)
  local copies, waits for them, and re-layouts  8.84 us (4%)
  other arithmetic  8.54 us (4%)
    ppermute x25, waiting for transfers between devices, send(): return lax.ppermute(array, ALL, route)  84.3 us
    pallas_call x6, Pallas kernels, weight_part(): pl.pallas_call(functools.partial(weight_body, len(pieces), final is not N...  34 us
    pallas_call x4, Pallas kernels, encoder_part(): pl.pallas_call(encoder_body, grid=(depth // TILE,), in_specs=[grad, grad,...  30.8 us
    ppermute x25, starting transfers between devices, send(): return lax.ppermute(array, ALL, route)  29.9 us
    pallas_call x4, Pallas kernels, project(): pl.pallas_call(project_body, grid=(4,), in_specs=[pl.BlockSpec((rows // 4...  26.6 us
    unnamed x24, local copies, waits for them, and re-layouts  7.39 us
    pallas_call x1, Pallas kernels, attend(): pl.pallas_call(attend_body, grid=(width // HEAD_DIM,), in_specs=[head, he...  7.03 us
  transfers between devices with their start and end apart: 25, of which 12 were waited for; matrix products, arithmetic and copies ran while one was open for 2% of the time, Pallas kernels for 30%

profile of v1, /device:TPU:0, one launch (start us, length us, event | category | flops | bytes accessed | tf_op | source)
XLA Modules:
  0.0 230.9 jit_solution(17158375423342699163)
XLA Ops:
  0.7 1.3 dynamic-slice_bitcast_fusion
  1.9 1.7 collective-permute-start
  3.6 7.6 %collective-permute-done.c.refs_4_ = bf16[64,4096]{1,0:T(8,128)(2,1)S(1)} collective-permute-done((bf16[64,4096]{1,0:T(8,128)(2,1)S(1)}, bf16[64,4096]{1,0:T(8,128)(2,1)S(1)}, u32[]{:S(2)}, u32[]{:S(2)}) %collective-permute-start) | collective-permute-done | bytes 524320 | tf_op jit(solution)/shard_map/ppermute | solution.py:57
  11.2 2.8 %collective-permute-start.4 = (bf16[64,4096]{1,0:T(8,128)(2,1)S(1)}, bf16[64,4096]{1,0:T(8,128)(2,1)S(1)}, u32[]{:S(2)}, u32[]{:S(2)}) collective-permute-start(bf16[64,4096]{1,0:T(8,128)(2,1)S(1)} %get-tuple-element.23.a.refs_0_), channel_id=1, source_target_pairs={{0,48},{4,20},{64,112},{68,84},{8,56},{12,28},{72,120},{76,92},{1,... | collective-permute-start | bytes 1572872 | tf_op jit(solution)/shard_map/ppermute | solution.py:57
  14.4 2.0 collective-permute-start.6
  16.4 1.9 collective-permute-start.2
  18.4 3.2 %collective-permute-done.4.c.refs_2_ = bf16[64,4096]{1,0:T(8,128)(2,1)S(1)} collective-permute-done((bf16[64,4096]{1,0:T(8,128)(2,1)S(1)}, bf16[64,4096]{1,0:T(8,128)(2,1)S(1)}, u32[]{:S(2)}, u32[]{:S(2)}) %collective-permute-start.4) | collective-permute-done | bytes 524320 | tf_op jit(solution)/shard_map/ppermute | solution.py:57
  21.6 2.0 collective-permute-start.10
  23.6 3.6 %collective-permute-done.8.c.refs_6_ = bf16[64,4096]{1,0:T(8,128)(2,1)S(1)} collective-permute-done((bf16[64,4096]{1,0:T(8,128)(2,1)S(1)}, bf16[64,4096]{1,0:T(8,128)(2,1)S(1)}, u32[]{:S(2)}, u32[]{:S(2)}) %collective-permute-start.8) | collective-permute-done | bytes 524320 | tf_op jit(solution)/shard_map/ppermute | solution.py:57
  27.2 2.0 collective-permute-start.12
  29.2 2.2 collective-permute-done.2.a.refs_1_
  32.7 4.2 %collective-permute-done.10.a.refs_3_ = bf16[64,4096]{1,0:T(8,128)(2,1)S(1)} collective-permute-done((bf16[64,4096]{1,0:T(8,128)(2,1)S(1)}, bf16[64,4096]{1,0:T(8,128)(2,1)S(1)}, u32[]{:S(2)}, u32[]{:S(2)}) %collective-permute-start.10) | collective-permute-done | bytes 524320 | tf_op jit(solution)/shard_map/ppermute | solution.py:57
  37.8 4.8 %collective-permute-done.12.c.refs_7_ = bf16[64,4096]{1,0:T(8,128)(2,1)} collective-permute-done((bf16[64,4096]{1,0:T(8,128)(2,1)S(1)}, bf16[64,4096]{1,0:T(8,128)(2,1)}, u32[]{:S(2)}, u32[]{:S(2)}) %collective-permute-start.12) | collective-permute-done | bytes 524320 | tf_op jit(solution)/shard_map/ppermute | solution.py:57
  43.2 1.0 copy-done.1
  44.2 6.4 %shard_map.75 = (bf16[256,512]{1,0:T(8,128)(2,1)S(1)}, bf16[256,512]{1,0:T(8,128)(2,1)S(1)}) custom-call(bf16[64,4096]{1,0:T(8,128)(2,1)S(1)} %get-tuple-element.23.a.refs_0_, bf16[64,4096]{1,0:T(8,128)(2,1)S(1)} %get-tuple-element.40.b.refs_8_, bf16[64,4096]{1,0:T(8,128)(2,1)S(1)} %collective-permute-done.c.refs_4_, bf16[64,4096]{1,0:T(8,128)(2,1)S(1)} %copy-done.1, ...), custom_call_target="tpu_custom_call" | custom-call | flops 2147483648 | bytes 10485760 | tf_op jit(solution)/shard_map/pallas_call | solution.py:87
  50.6 6.6 %shard_map.77 = (bf16[256,512]{1,0:T(8,128)(2,1)S(1)}, bf16[256,512]{1,0:T(8,128)(2,1)S(1)}) custom-call(bf16[64,4096]{1,0:T(8,128)(2,1)S(1)} %collective-permute-done.6.a.refs_5_, bf16[64,4096]{1,0:T(8,128)(2,1)} %collective-permute-done.7.b.refs_13_, bf16[64,4096]{1,0:T(8,128)(2,1)S(1)} %collective-permute-done.8.c.refs_6_, ...), custom_call_target="tpu_custom_call" | custom-call | flops 2147483648 | bytes 10485760 | tf_op jit(solution)/shard_map/pallas_call | solution.py:87
  57.3 6.7 %shard_map.76 = (bf16[256,512]{1,0:T(8,128)(2,1)S(1)}, bf16[256,512]{1,0:T(8,128)(2,1)S(1)}) custom-call(bf16[64,4096]{1,0:T(8,128)(2,1)} %collective-permute-done.2.a.refs_1_, bf16[64,4096]{1,0:T(8,128)(2,1)} %collective-permute-done.3.b.refs_9_, bf16[64,4096]{1,0:T(8,128)(2,1)S(1)} %collective-permute-done.4.c.refs_2_, ...), custom_call_target="tpu_custom_call" | custom-call | flops 2147483648 | bytes 10485760 | tf_op jit(solution)/shard_map/pallas_call | solution.py:87
  64.0 6.9 %shard_map.78 = (bf16[256,512]{1,0:T(8,128)(2,1)S(1)}, bf16[256,512]{1,0:T(8,128)(2,1)S(1)}) custom-call(bf16[64,4096]{1,0:T(8,128)(2,1)S(1)} %copy-done.3, bf16[64,4096]{1,0:T(8,128)(2,1)S(1)} %collective-permute-done.11.b.refs_11_, bf16[64,4096]{1,0:T(8,128)(2,1)} %collective-permute-done.12.c.refs_7_, ...), custom_call_target="tpu_custom_call" | custom-call | flops 2147483648 | bytes 10485760 | tf_op jit(solution)/shard_map/pallas_call | solution.py:87
  71.0 7.0 %shard_map.79 = (bf16[1,1,512,512]{3,2,1,0:T(8,128)(2,1)}, bf16[1,1,512,512]{3,2,1,0:T(8,128)(2,1)}, bf16[1024,512]{1,0:T(8,128)(2,1)S(1)}, bf16[1024,512]{1,0:T...) custom-call(bf16[1,1,512,512]{3,2,1,0:T(8,128)(2,1)S(1)} %copy-done.8, ...), custom_call_target="tpu_custom_call" | custom-call | flops 3221225472 | bytes 8388608 | tf_op jit(solution)/shard_map/pallas_call | solution.py:154
  78.0 6.9 %shard_map.80 = bf16[512,2048]{1,0:T(8,128)(2,1)} custom-call(s32[4]{0:T(128)S(1)} %pad_add_fusion.index, bf16[512,1024]{1,0:T(8,128)(2,1)} %get-tuple-element.35.grad_t, bf16[64,4096]{1,0:T(8,128)(2,1)S(1)} %get-tuple-element.23.a.refs_0_, bf16[64,4096]{1,0:T(8,128)(2,1)} %collective-permute-done.2.a.refs_1_, ...), custom_call_target="tpu_custom_call" | custom-call | flops 2147483648 | bytes 8388608 | tf_op jit(solution)/shard_map/pallas_call | solution.py:206
  84.9 7.6 %shard_map.83 = bf16[256,4096]{1,0:T(8,128)(2,1)S(1)} custom-call(bf16[1024,512]{1,0:T(8,128)(2,1)S(1)} %get-tuple-element.36.kg, bf16[1024,512]{1,0:T(8,128)(2,1)S(1)} %get-tuple-element.37.vg, bf16[1,2,4096,512]{3,2,1,0:T(8,128)(2,1)} %w.15), custom_call_target="tpu_custom_call" | custom-call | flops 2147483648 | bytes 12582912 | tf_op jit(solution)/shard_map/pallas_call | solution.py:233
  92.6 7.6 %shard_map.81 = bf16[256,4096]{1,0:T(8,128)(2,1)S(1)} custom-call(bf16[1024,512]{1,0:T(8,128)(2,1)S(1)} %get-tuple-element.36.kg, bf16[1024,512]{1,0:T(8,128)(2,1)S(1)} %get-tuple-element.37.vg, bf16[1,2,4096,512]{3,2,1,0:T(8,128)(2,1)} %w.15), custom_call_target="tpu_custom_call" | custom-call | flops 2147483648 | bytes 12582912 | tf_op jit(solution)/shard_map/pallas_call | solution.py:233
  100.9 1.3 copy-done.11
  102.2 7.8 %shard_map.84 = bf16[256,4096]{1,0:T(8,128)(2,1)S(1)} custom-call(bf16[1024,512]{1,0:T(8,128)(2,1)S(1)} %get-tuple-element.36.kg, bf16[1024,512]{1,0:T(8,128)(2,1)S(1)} %get-tuple-element.37.vg, bf16[1,2,4096,512]{3,2,1,0:T(8,128)(2,1)} %w.15, bf16[256,4096]{1,0:T(8,128)(2,1)} %copy-done.11), custom_call_target="tpu_custom_call" | custom-call | flops 2147483648 | bytes 12582912 | tf_op jit(solution)/shard_map/pallas_call | solution.py:233
  110.4 1.3 copy-done.10
  111.7 7.8 %shard_map.82 = bf16[256,4096]{1,0:T(8,128)(2,1)S(1)} custom-call(bf16[1024,512]{1,0:T(8,128)(2,1)S(1)} %get-tuple-element.36.kg, bf16[1024,512]{1,0:T(8,128)(2,1)S(1)} %get-tuple-element.37.vg, bf16[1,2,4096,512]{3,2,1,0:T(8,128)(2,1)} %w.15, bf16[256,4096]{1,0:T(8,128)(2,1)} %copy-done.10), custom_call_target="tpu_custom_call" | custom-call | flops 2147483648 | bytes 12582912 | tf_op jit(solution)/shard_map/pallas_call | solution.py:233
  119.6 16.7 %collective-permute-done.16 = bf16[256,4096]{1,0:T(8,128)(2,1)} collective-permute-done((bf16[256,4096]{1,0:T(8,128)(2,1)S(1)}, bf16[256,4096]{1,0:T(8,128)(2,1)}, u32[]{:S(2)}, u32[]{:S(2)}) %collective-permute-start.16) | collective-permute-done | bytes 2097184 | tf_op jit(solution)/shard_map/ppermute | solution.py:57
  136.3 2.3 convert_add_fusion
  138.7 2.8 %collective-permute-start.17 = (bf16[128,4096]{1,0:T(8,128)(2,1)S(1)}, bf16[128,4096]{1,0:T(8,128)(2,1)S(1)}, u32[]{:S(2)}, u32[]{:S(2)}) collective-permute-start(bf16[128,4096]{1,0:T(8,128)(2,1)S(1)} %slice.28), channel_id=1, source_target_pairs={{0,48},{4,20},{64,112},{68,84},{8,56},{12,28},{72,120},{76,92},{1,... | collective-permute-start | bytes 3145736 | tf_op jit(solution)/shard_map/ppermute | solution.py:57
  141.5 1.6 collective-permute-start.23
  143.1 6.8 %shard_map.85 = bf16[512,2048]{1,0:T(8,128)(2,1)} custom-call(s32[4]{0:T(128)S(1)} %pad_add_fusion.index, bf16[512,1024]{1,0:T(8,128)(2,1)} %get-tuple-element.39.grad_t, bf16[64,4096]{1,0:T(8,128)(2,1)S(1)} %get-tuple-element.23.a.refs_0_, bf16[64,4096]{1,0:T(8,128)(2,1)} %collective-permute-done.2.a.refs_1_, ...), custom_call_target="tpu_custom_call" | custom-call | flops 2147483648 | bytes 8388608 | tf_op jit(solution)/shard_map/pallas_call | solution.py:206
  150.4 4.4 %collective-permute-done.17 = bf16[128,4096]{1,0:T(8,128)(2,1)S(1)} collective-permute-done((bf16[128,4096]{1,0:T(8,128)(2,1)S(1)}, bf16[128,4096]{1,0:T(8,128)(2,1)S(1)}, u32[]{:S(2)}, u32[]{:S(2)}) %collective-permute-start.17) | collective-permute-done | bytes 1048608 | tf_op jit(solution)/shard_map/ppermute | solution.py:57
  155.1 2.1 collective-permute-start.18
  157.2 7.2 %collective-permute-done.18 = bf16[64,4096]{1,0:T(8,128)(2,1)S(1)} collective-permute-done((bf16[64,4096]{1,0:T(8,128)(2,1)S(1)}, bf16[64,4096]{1,0:T(8,128)(2,1)S(1)}, u32[]{:S(2)}, u32[]{:S(2)}) %collective-permute-start.18) | collective-permute-done | bytes 524320 | tf_op jit(solution)/shard_map/ppermute | solution.py:57
  164.3 0.9 fusion
  165.2 1.9 collective-permute-start.19
  167.9 1.0 copy-done.4
  168.9 4.9 %shard_map.87 = bf16[512,1024]{1,0:T(8,128)(2,1)} custom-call(s32[2]{0:T(128)S(1)} %pad_add_fusion.2.index, bf16[512,1024]{1,0:T(8,128)(2,1)} %get-tuple-element.35.grad_t, bf16[64,4096]{1,0:T(8,128)(2,1)S(1)} %get-tuple-element.23.a.refs_0_, bf16[64,4096]{1,0:T(8,128)(2,1)} %collective-permute-done.2.a.refs_1_, ...), custom_call_target="tpu_custom_call" | custom-call | flops 1073741824 | bytes 4194304 | tf_op jit(solution)/shard_map/pallas_call | solution.py:206
  173.9 3.0 %collective-permute-start.24 = (bf16[512,1024]{1,0:T(8,128)(2,1)}, bf16[512,1024]{1,0:T(8,128)(2,1)}, u32[]{:S(2)}, u32[]{:S(2)}) collective-permute-start(bf16[512,1024]{1,0:T(8,128)(2,1)} %shard_map.87), channel_id=1, source_target_pairs={{0,3},{4,5},{64,67},{68,69},{8,11},{12,13},{72,75},{76,77},{1,2},{... | collective-permute-start | bytes 3145736 | tf_op jit(solution)/shard_map/ppermute | solution.py:57
  176.9 24.7 %collective-permute-done.21.refs_16_ = bf16[512,2048]{1,0:T(8,128)(2,1)} collective-permute-done((bf16[512,2048]{1,0:T(8,128)(2,1)}, bf16[512,2048]{1,0:T(8,128)(2,1)}, u32[]{:S(2)}, u32[]{:S(2)}) %collective-permute-start.21) | collective-permute-done | bytes 2097184 | tf_op jit(solution)/shard_map/ppermute | solution.py:57
  201.6 4.9 %shard_map.86 = bf16[512,1024]{1,0:T(8,128)(2,1)} custom-call(s32[2]{0:T(128)S(1)} %pad_add_fusion.2.index, bf16[512,1024]{1,0:T(8,128)(2,1)} %get-tuple-element.39.grad_t, bf16[64,4096]{1,0:T(8,128)(2,1)S(1)} %get-tuple-element.23.a.refs_0_, bf16[64,4096]{1,0:T(8,128)(2,1)} %collective-permute-done.2.a.refs_1_, ...), custom_call_target="tpu_custom_call" | custom-call | flops 1073741824 | bytes 4194304 | tf_op jit(solution)/shard_map/pallas_call | solution.py:206
  206.5 3.0 %collective-permute-start.22 = (bf16[512,1024]{1,0:T(8,128)(2,1)}, bf16[512,1024]{1,0:T(8,128)(2,1)}, u32[]{:S(2)}, u32[]{:S(2)}) collective-permute-start(bf16[512,1024]{1,0:T(8,128)(2,1)} %shard_map.86), channel_id=1, source_target_pairs={{0,3},{4,5},{64,67},{68,69},{8,11},{12,13},{72,75},{76,77},{1,2},{... | collective-permute-start | bytes 3145736 | tf_op jit(solution)/shard_map/ppermute | solution.py:57
  209.5 2.1 add_convert_fusion
  211.8 1.0 copy-done.5
  212.8 5.2 %shard_map.88.refs_18_ = bf16[1,2,1024,512]{3,2,1,0:T(8,128)(2,1)} custom-call(s32[2]{0:T(128)S(1)} %pad_add_fusion.1.index, bf16[512,1024]{1,0:T(8,128)(2,1)} %get-tuple-element.35.grad_t, bf16[64,4096]{1,0:T(8,128)(2,1)S(1)} %get-tuple-element.23.a.refs_0_, bf16[64,4096]{1,0:T(8,128)(2,1)} %collective-permute-done.2.a.refs_1_, ...), custom_call_target="tpu_custom_call" | custom-call | flops 1073741824 | bytes 4194304 | tf_op jit(solution)/shard_map/pallas_call | solution.py:206
  218.0 4.8 %collective-permute-done.22.refs_17_ = bf16[512,1024]{1,0:T(8,128)(2,1)} collective-permute-done((bf16[512,1024]{1,0:T(8,128)(2,1)}, bf16[512,1024]{1,0:T(8,128)(2,1)}, u32[]{:S(2)}, u32[]{:S(2)}) %collective-permute-start.22) | collective-permute-done | bytes 1048608 | tf_op jit(solution)/shard_map/ppermute | solution.py:57
  222.9 5.2 %shard_map.89 = bf16[1,2,1024,512]{3,2,1,0:T(8,128)(2,1)} custom-call(s32[2]{0:T(128)S(1)} %pad_add_fusion.1.index, bf16[512,1024]{1,0:T(8,128)(2,1)} %get-tuple-element.39.grad_t, bf16[64,4096]{1,0:T(8,128)(2,1)S(1)} %get-tuple-element.23.a.refs_0_, bf16[64,4096]{1,0:T(8,128)(2,1)} %collective-permute-done.2.a.refs_1_, ...), custom_call_target="tpu_custom_call", output_to_operand_aliasing={{}: (20, {})} | custom-call | flops 1073741824 | bytes 4194304 | tf_op jit(solution)/shard_map/pallas_call | solution.py:206
  228.1 2.8 %maximum_select_fusion = bf16[1,128,4096]{2,1,0:T(8,128)(2,1)} fusion(bf16[1,64,4096]{2,1,0:T(8,128)(2,1)} %bitcast.7, bf16[1,64,4096]{2,1,0:T(8,128)(2,1)} %bitcast.6, pred[]{:T(512)S(6)} %eq.8), kind=kLoop, calls=%fused_computation.6 | loop fusion | flops 4718592 | bytes 2097153 | tf_op jit(solution)/shard_map/jit(_where)/select_n | solution.py:313
  (52 shorter events, 6.1 us)
Async XLA Ops:
  1.9 9.3 %collective-permute-start = (bf16[64,4096]{1,0:T(8,128)(2,1)S(1)}, bf16[64,4096]{1,0:T(8,128)(2,1)S(1)}, u32[]{:S(2)}, u32[]{:S(2)}) collective-permute-start(bf16[64,4096]{1,0:T(8,128)(2,1)S(1)} %get-tuple-element.23.a.refs_0_), channel_id=1, source_target_pairs={{0,16},{4,52},{64,80},{68,116},{8,24},{12,60},{72,88},{76,124},{1,... | collective-permute-start | bytes 1572872 | tf_op jit(solution)/shard_map/ppermute | solution.py:57
  11.2 10.4 %collective-permute-start.4 = (bf16[64,4096]{1,0:T(8,128)(2,1)S(1)}, bf16[64,4096]{1,0:T(8,128)(2,1)S(1)}, u32[]{:S(2)}, u32[]{:S(2)}) collective-permute-start(bf16[64,4096]{1,0:T(8,128)(2,1)S(1)} %get-tuple-element.23.a.refs_0_), channel_id=1, source_target_pairs={{0,48},{4,20},{64,112},{68,84},{8,56},{12,28},{72,120},{76,92},{1,... | collective-permute-start | bytes 1572872 | tf_op jit(solution)/shard_map/ppermute | solution.py:57
  14.0 13.2 %collective-permute-start.8 = (bf16[64,4096]{1,0:T(8,128)(2,1)S(1)}, bf16[64,4096]{1,0:T(8,128)(2,1)S(1)}, u32[]{:S(2)}, u32[]{:S(2)}) collective-permute-start(bf16[64,4096]{1,0:T(8,128)(2,1)S(1)} %collective-permute-done.c.refs_4_), channel_id=1, source_target_pairs={{0,48},{4,20},{64,112},{68,84},{8,56},{12,28},{72,120},{76,92},{1,... | collective-permute-start | bytes 1572872 | tf_op jit(solution)/shard_map/ppermute | solution.py:57
  14.4 14.8 %collective-permute-start.6 = (bf16[64,4096]{1,0:T(8,128)(2,1)S(1)}, bf16[64,4096]{1,0:T(8,128)(2,1)S(1)}, u32[]{:S(2)}, u32[]{:S(2)}) collective-permute-start(bf16[64,4096]{1,0:T(8,128)(2,1)S(1)} %collective-permute-done.c.refs_4_), channel_id=1, source_target_pairs={{0,64},{4,76},{64,8},{68,4},{8,72},{12,68},{72,0},{76,12},{1,65},{... | collective-permute-start | bytes 1572872 | tf_op jit(solution)/shard_map/ppermute | solution.py:57
  16.4 15.0 %collective-permute-start.2 = (bf16[64,4096]{1,0:T(8,128)(2,1)S(1)}, bf16[64,4096]{1,0:T(8,128)(2,1)}, u32[]{:S(2)}, u32[]{:S(2)}) collective-permute-start(bf16[64,4096]{1,0:T(8,128)(2,1)S(1)} %get-tuple-element.23.a.refs_0_), channel_id=1, source_target_pairs={{0,64},{4,76},{64,8},{68,4},{8,72},{12,68},{72,0},{76,12},{1,65},{... | collective-permute-start | bytes 1572872 | tf_op jit(solution)/shard_map/ppermute | solution.py:57
  18.3 13.1 %collective-permute-start.1 = (bf16[64,4096]{1,0:T(8,128)(2,1)S(1)}, bf16[64,4096]{1,0:T(8,128)(2,1)S(1)}, u32[]{:S(2)}, u32[]{:S(2)}) collective-permute-start(bf16[64,4096]{1,0:T(8,128)(2,1)S(1)} %collective-permute-done.c.refs_4_), channel_id=1, source_target_pairs={{0,4},{4,0},{64,68},{68,64},{8,12},{12,8},{72,76},{76,72},{1,5},{5... | collective-permute-start | bytes 1572872 | tf_op jit(solution)/shard_map/ppermute | solution.py:57
  21.6 15.4 %collective-permute-start.10 = (bf16[64,4096]{1,0:T(8,128)(2,1)S(1)}, bf16[64,4096]{1,0:T(8,128)(2,1)S(1)}, u32[]{:S(2)}, u32[]{:S(2)}) collective-permute-start(bf16[64,4096]{1,0:T(8,128)(2,1)S(1)} %collective-permute-done.4.c.refs_2_), channel_id=1, source_target_pairs={{0,64},{4,76},{64,8},{68,4},{8,72},{12,68},{72,0},{76,12},{1,65},{... | collective-permute-start | bytes 1572872 | tf_op jit(solution)/shard_map/ppermute | solution.py:57
  27.2 15.5 %collective-permute-start.12 = (bf16[64,4096]{1,0:T(8,128)(2,1)S(1)}, bf16[64,4096]{1,0:T(8,128)(2,1)}, u32[]{:S(2)}, u32[]{:S(2)}) collective-permute-start(bf16[64,4096]{1,0:T(8,128)(2,1)S(1)} %collective-permute-done.8.c.refs_6_), channel_id=1, source_target_pairs={{0,64},{4,76},{64,8},{68,4},{8,72},{12,68},{72,0},{76,12},{1,65},{... | collective-permute-start | bytes 1572872 | tf_op jit(solution)/shard_map/ppermute | solution.py:57
  29.2 13.5 %collective-permute-start.7 = (bf16[64,4096]{1,0:T(8,128)(2,1)S(1)}, bf16[64,4096]{1,0:T(8,128)(2,1)}, u32[]{:S(2)}, u32[]{:S(2)}) collective-permute-start(bf16[64,4096]{1,0:T(8,128)(2,1)S(1)} %collective-permute-done.6.a.refs_5_), channel_id=1, source_target_pairs={{0,4},{4,0},{64,68},{68,64},{8,12},{12,8},{72,76},{76,72},{1,5},{5... | collective-permute-start | bytes 1572872 | tf_op jit(solution)/shard_map/ppermute | solution.py:57
  31.4 19.2 %collective-permute-start.9 = (bf16[64,4096]{1,0:T(8,128)(2,1)S(1)}, bf16[64,4096]{1,0:T(8,128)(2,1)}, u32[]{:S(2)}, u32[]{:S(2)}) collective-permute-start(bf16[64,4096]{1,0:T(8,128)(2,1)S(1)} %collective-permute-done.8.c.refs_6_), channel_id=1, source_target_pairs={{0,4},{4,0},{64,68},{68,64},{8,12},{12,8},{72,76},{76,72},{1,5},{5... | collective-permute-start | bytes 1572872 | tf_op jit(solution)/shard_map/ppermute | solution.py:57
  31.4 0.8 copy-start
  32.2 25.0 %collective-permute-start.3 = (bf16[64,4096]{1,0:T(8,128)(2,1)}, bf16[64,4096]{1,0:T(8,128)(2,1)}, u32[]{:S(2)}, u32[]{:S(2)}) collective-permute-start(bf16[64,4096]{1,0:T(8,128)(2,1)} %collective-permute-done.2.a.refs_1_), channel_id=1, source_target_pairs={{0,4},{4,0},{64,68},{68,64},{8,12},{12,8},{72,76},{76,72},{1,5},{5... | collective-permute-start | bytes 1572872 | tf_op jit(solution)/shard_map/ppermute | solution.py:57
  36.9 0.8 copy-start.2
  37.7 19.5 %collective-permute-start.5 = (bf16[64,4096]{1,0:T(8,128)(2,1)S(1)}, bf16[64,4096]{1,0:T(8,128)(2,1)}, u32[]{:S(2)}, u32[]{:S(2)}) collective-permute-start(bf16[64,4096]{1,0:T(8,128)(2,1)S(1)} %collective-permute-done.4.c.refs_2_), channel_id=1, source_target_pairs={{0,4},{4,0},{64,68},{68,64},{8,12},{12,8},{72,76},{76,72},{1,5},{5... | collective-permute-start | bytes 1572872 | tf_op jit(solution)/shard_map/ppermute | solution.py:57
  42.7 21.3 %collective-permute-start.11 = (bf16[64,4096]{1,0:T(8,128)(2,1)}, bf16[64,4096]{1,0:T(8,128)(2,1)S(1)}, u32[]{:S(2)}, u32[]{:S(2)}) collective-permute-start(bf16[64,4096]{1,0:T(8,128)(2,1)} %copy-done.2), channel_id=1, source_target_pairs={{0,4},{4,0},{64,68},{68,64},{8,12},{12,8},{72,76},{76,72},{1,5},{5... | collective-permute-start | bytes 1572872 | tf_op jit(solution)/shard_map/ppermute | solution.py:57
  42.7 21.3 %collective-permute-start.13 = (bf16[64,4096]{1,0:T(8,128)(2,1)}, bf16[64,4096]{1,0:T(8,128)(2,1)S(1)}, u32[]{:S(2)}, u32[]{:S(2)}) collective-permute-start(bf16[64,4096]{1,0:T(8,128)(2,1)} %collective-permute-done.12.c.refs_7_), channel_id=1, source_target_pairs={{0,4},{4,0},{64,68},{68,64},{8,12},{12,8},{72,76},{76,72},{1,5},{5... | collective-permute-start | bytes 1572872 | tf_op jit(solution)/shard_map/ppermute | solution.py:57
  43.2 1.0 copy-start.1
  57.2 6.8 %copy-start.3 = (bf16[64,4096]{1,0:T(8,128)(2,1)S(1)}, bf16[64,4096]{1,0:T(8,128)(2,1)}, u32[]{:S(2)}) copy-start(bf16[64,4096]{1,0:T(8,128)(2,1)} %copy-done.2) | copy-start | bytes 1572868
  64.0 7.0 %copy-start.8 = (bf16[1,1,512,512]{3,2,1,0:T(8,128)(2,1)S(1)}, bf16[1,1,512,512]{3,2,1,0:T(8,128)(2,1)}, u32[]{:S(2)}) copy-start(bf16[1,1,512,512]{3,2,1,0:T(8,128)(2,1)} %q.1) | copy-start | bytes 1572868
  64.0 7.0 %copy-start.9 = (bf16[1,1,512,512]{3,2,1,0:T(8,128)(2,1)S(1)}, bf16[1,1,512,512]{3,2,1,0:T(8,128)(2,1)}, u32[]{:S(2)}) copy-start(bf16[1,1,512,512]{3,2,1,0:T(8,128)(2,1)} %g.1) | copy-start | bytes 1572868
  64.0 7.0 %copy-start.6 = (bf16[64,4096]{1,0:T(8,128)(2,1)}, bf16[64,4096]{1,0:T(8,128)(2,1)S(1)}, u32[]{:S(2)}) copy-start(bf16[64,4096]{1,0:T(8,128)(2,1)S(1)} %collective-permute-done.11.b.refs_11_) | copy-start | bytes 1572868
  64.0 6.9 %copy-start.7 = (bf16[64,4096]{1,0:T(8,128)(2,1)}, bf16[64,4096]{1,0:T(8,128)(2,1)S(1)}, u32[]{:S(2)}) copy-start(bf16[64,4096]{1,0:T(8,128)(2,1)S(1)} %collective-permute-done.13.d.refs_15_) | copy-start | bytes 1572868
  92.5 8.4 %collective-permute-start.15 = (bf16[256,4096]{1,0:T(8,128)(2,1)S(1)}, bf16[256,4096]{1,0:T(8,128)(2,1)S(1)}, u32[]{:S(2)}, u32[]{:S(2)}) collective-permute-start(bf16[256,4096]{1,0:T(8,128)(2,1)S(1)} %shard_map.83), channel_id=1, source_target_pairs={{0,4},{4,0},{64,68},{68,64},{8,12},{12,8},{72,76},{76,72},{1,5},{5... | collective-permute-start | bytes 6291464 | tf_op jit(solution)/shard_map/ppermute | solution.py:57
  100.1 10.3 %collective-permute-start.14 = (bf16[256,4096]{1,0:T(8,128)(2,1)S(1)}, bf16[256,4096]{1,0:T(8,128)(2,1)S(1)}, u32[]{:S(2)}, u32[]{:S(2)}) collective-permute-start(bf16[256,4096]{1,0:T(8,128)(2,1)S(1)} %shard_map.81), channel_id=1, source_target_pairs={{0,4},{4,0},{64,68},{68,64},{8,12},{12,8},{72,76},{76,72},{1,5},{5... | collective-permute-start | bytes 6291464 | tf_op jit(solution)/shard_map/ppermute | solution.py:57
  100.9 1.3 copy-start.11
  110.1 26.2 %collective-permute-start.16 = (bf16[256,4096]{1,0:T(8,128)(2,1)S(1)}, bf16[256,4096]{1,0:T(8,128)(2,1)}, u32[]{:S(2)}, u32[]{:S(2)}) collective-permute-start(bf16[256,4096]{1,0:T(8,128)(2,1)S(1)} %shard_map.84), channel_id=1, source_target_pairs={{0,16},{4,52},{64,80},{68,116},{8,24},{12,60},{72,88},{76,124},{1,... | collective-permute-start | bytes 6291464 | tf_op jit(solution)/shard_map/ppermute | solution.py:57
  110.4 1.3 copy-start.10
  138.7 16.1 %collective-permute-start.17 = (bf16[128,4096]{1,0:T(8,128)(2,1)S(1)}, bf16[128,4096]{1,0:T(8,128)(2,1)S(1)}, u32[]{:S(2)}, u32[]{:S(2)}) collective-permute-start(bf16[128,4096]{1,0:T(8,128)(2,1)S(1)} %slice.28), channel_id=1, source_target_pairs={{0,48},{4,20},{64,112},{68,84},{8,56},{12,28},{72,120},{76,92},{1,... | collective-permute-start | bytes 3145736 | tf_op jit(solution)/shard_map/ppermute | solution.py:57
  141.5 26.4 %collective-permute-start.23 = (bf16[512,2048]{1,0:T(8,128)(2,1)}, bf16[512,2048]{1,0:T(8,128)(2,1)}, u32[]{:S(2)}, u32[]{:S(2)}) collective-permute-start(bf16[512,2048]{1,0:T(8,128)(2,1)} %shard_map.80), channel_id=1, source_target_pairs={{0,1},{4,7},{64,65},{68,71},{8,9},{12,15},{72,73},{76,79},{1,0},{5... | collective-permute-start | bytes 6291464 | tf_op jit(solution)/shard_map/ppermute | solution.py:57
  149.9 51.7 %collective-permute-start.21 = (bf16[512,2048]{1,0:T(8,128)(2,1)}, bf16[512,2048]{1,0:T(8,128)(2,1)}, u32[]{:S(2)}, u32[]{:S(2)}) collective-permute-start(bf16[512,2048]{1,0:T(8,128)(2,1)} %shard_map.85), channel_id=1, source_target_pairs={{0,1},{4,7},{64,65},{68,71},{8,9},{12,15},{72,73},{76,79},{1,0},{5... | collective-permute-start | bytes 6291464 | tf_op jit(solution)/shard_map/ppermute | solution.py:57
  155.1 9.3 %collective-permute-start.18 = (bf16[64,4096]{1,0:T(8,128)(2,1)S(1)}, bf16[64,4096]{1,0:T(8,128)(2,1)S(1)}, u32[]{:S(2)}, u32[]{:S(2)}) collective-permute-start(bf16[64,4096]{1,0:T(8,128)(2,1)S(1)} %slice.29), channel_id=1, source_target_pairs={{0,72},{4,68},{64,0},{68,12},{8,64},{12,76},{72,8},{76,4},{1,73},{... | collective-permute-start | bytes 1572872 | tf_op jit(solution)/shard_map/ppermute | solution.py:57
  165.2 44.3 %collective-permute-start.19 = (bf16[64,4096]{1,0:T(8,128)(2,1)}, bf16[64,4096]{1,0:T(8,128)(2,1)}, u32[]{:S(2)}, u32[]{:S(2)}) collective-permute-start(bf16[64,4096]{1,0:T(8,128)(2,1)} %fusion), channel_id=1, source_target_pairs={{0,8},{4,12},{64,72},{68,76},{8,0},{12,4},{72,64},{76,68},{1,9},{5... | collective-permute-start | bytes 1572872 | tf_op jit(solution)/shard_map/ppermute | solution.py:57
  167.9 1.0 copy-start.4
  173.9 37.9 %collective-permute-start.24 = (bf16[512,1024]{1,0:T(8,128)(2,1)}, bf16[512,1024]{1,0:T(8,128)(2,1)}, u32[]{:S(2)}, u32[]{:S(2)}) collective-permute-start(bf16[512,1024]{1,0:T(8,128)(2,1)} %shard_map.87), channel_id=1, source_target_pairs={{0,3},{4,5},{64,67},{68,69},{8,11},{12,13},{72,75},{76,77},{1,2},{... | collective-permute-start | bytes 3145736 | tf_op jit(solution)/shard_map/ppermute | solution.py:57
  206.5 16.3 %collective-permute-start.22 = (bf16[512,1024]{1,0:T(8,128)(2,1)}, bf16[512,1024]{1,0:T(8,128)(2,1)}, u32[]{:S(2)}, u32[]{:S(2)}) collective-permute-start(bf16[512,1024]{1,0:T(8,128)(2,1)} %shard_map.86), channel_id=1, source_target_pairs={{0,3},{4,5},{64,67},{68,69},{8,11},{12,13},{72,75},{76,77},{1,2},{... | collective-permute-start | bytes 3145736 | tf_op jit(solution)/shard_map/ppermute | solution.py:57
  211.7 16.4 %collective-permute-start.20 = (bf16[64,4096]{1,0:T(8,128)(2,1)}, bf16[64,4096]{1,0:T(8,128)(2,1)}, u32[]{:S(2)}, u32[]{:S(2)}) collective-permute-start(bf16[64,4096]{1,0:T(8,128)(2,1)} %add_convert_fusion), channel_id=1, source_target_pairs={{0,4},{4,0},{64,68},{68,64},{8,12},{12,8},{72,76},{76,72},{1,5},{5... | collective-permute-start | bytes 1572872 | tf_op jit(solution)/shard_map/ppermute | solution.py:57
  211.8 1.0 copy-start.5

commit v2 on v0

v2 whole, which is shorter than its diff:
```python
import functools

import jax
import jax.numpy as jnp
from jax import lax
from jax.experimental import pallas as pl
from jax.experimental.pallas import tpu as pltpu
from jax.sharding import PartitionSpec as P

HEAD_DIM = 256
ALL = ("pipe", "tensor", "dp")
F32, BF16 = jnp.float32, jnp.bfloat16
NT = (((1,), (1,)), ((), ()))
TN = (((0,), (0,)), ((), ()))
TILE = 512
WHOLE = pl.BlockSpec(memory_space=pltpu.VMEM)
SCALARS = pl.BlockSpec(memory_space=pltpu.SMEM)


def call(body, operands, shapes, scratch=(), index=0):
    many = isinstance(shapes, (list, tuple))
    return pl.pallas_call(
        body,
        in_specs=[SCALARS] * index + [WHOLE] * (len(operands) - index),
        out_specs=[WHOLE] * len(shapes) if many else WHOLE,
        out_shape=shapes,
        scratch_shapes=scratch,
        compiler_params=pltpu.CompilerParams(vmem_limit_bytes=20 * 1024 * 1024),
        cost_estimate=pl.CostEstimate(flops=1000, bytes_accessed=1000, transcendentals=0),
    )(*operands)


def bf16(*shape):
    return jax.ShapeDtypeStruct(shape, BF16)


def pairs(move):
    def index(x, y, z, core):
        pipe = (z % 2) * 4 + x
        tensor = (z // 2) * 2 + core
        return (pipe * 4 + tensor) * 4 + y

    found = []
    for x in range(4):
        for y in range(4):
            for z in range(4):
                for core in range(2):
                    to_x, to_y, to_z, to_core = move(x, y, z, core)
                    found.append((index(x, y, z, core), index(to_x, to_y, to_z % 4, to_core)))
    return found


def partner(place, core, which):
    return place ^ 1 if core == which else 3 - place


X_FIRST = pairs(lambda x, y, z, core: (partner(x, core, 0), y, z, core))
X_SECOND = pairs(lambda x, y, z, core: (partner(x, core, 1), y, z, core))
Y_FIRST = pairs(lambda x, y, z, core: (x, partner(y, core, 0), z, core))
Y_SECOND = pairs(lambda x, y, z, core: (x, partner(y, core, 1), z, core))
ALONG_Z = pairs(lambda x, y, z, core: (x, y, z + 1 - 2 * core, core))
BACK_Z = pairs(lambda x, y, z, core: (x, y, z - 1 + 2 * core, core))
ACROSS_Z = pairs(lambda x, y, z, core: (x, y, z + 2, core))
SWAP = pairs(lambda x, y, z, core: (x, y, z, 1 - core))


def send(array, route):
    return lax.ppermute(array, ALL, route)


def project_body(a, b, c, d, w, keys, values):
    x = jnp.concatenate([a[...], b[...], c[...], d[...]], 0)
    keys[...] = jnp.dot(x, w[0, 0], preferred_element_type=F32).astype(BF16)
    values[...] = jnp.dot(x, w[0, 1], preferred_element_type=F32).astype(BF16)


def project(pieces, kv_weight):
    shape = bf16(4 * pieces[0].shape[0], kv_weight.shape[3])
    return call(project_body, [*pieces, kv_weight], [shape, shape])


def arrange(groups):
    quarter = groups[0].shape[0] // 4

    def at(group, place):
        return groups[group][place * quarter : (place + 1) * quarter, :]

    order = [(0, 0), (1, 0), (1, 2), (3, 0), (0, 2), (2, 0), (2, 2), (3, 2)]
    return jnp.concatenate(
        [at(g, p) for g, p in order] + [at(g, p + 1) for g, p in order], 0
    )


def attend_body(q, g, k0, k1, k2, k3, v0, v1, v2, v3, att, dq, kg, vg, kgt, vgt, low, dlow):
    scale = HEAD_DIM ** (-0.5)
    total = q.shape[2]
    chunk = total // 2
    for head in range(q.shape[3] // HEAD_DIM):
        cols = slice(head * HEAD_DIM, (head + 1) * HEAD_DIM)
        k = arrange([ref[:, cols] for ref in (k0, k1, k2, k3)])
        v = arrange([ref[:, cols] for ref in (v0, v1, v2, v3)])
        for part in range(2):
            rows = slice(part * chunk, (part + 1) * chunk)
            g_rows = g[0, 0, rows, cols]
            scores = scale * lax.dot_general(
                q[0, 0, rows, cols], k, NT, preferred_element_type=F32
            )
            expd = jnp.exp(scores - jnp.max(scores, axis=-1, keepdims=True))
            probs = expd * (1.0 / jnp.sum(expd, axis=-1, keepdims=True))
            probs_low = probs.astype(BF16)
            low[head, rows, :] = probs_low
            out = jnp.dot(probs_low, v, preferred_element_type=F32).astype(BF16)
            att[0, 0, rows, cols] = out
            dprobs = lax.dot_general(g_rows, v, NT, preferred_element_type=F32)
            delta = jnp.sum(g_rows.astype(F32) * out.astype(F32), axis=-1, keepdims=True)
            ds_low = (probs * (dprobs - delta)).astype(BF16)
            dlow[head, rows, :] = ds_low
            dq[0, 0, rows, cols] = (
                scale * jnp.dot(ds_low, k, preferred_element_type=F32)
            ).astype(BF16)
        value_t = lax.dot_general(g[0, 0, :, cols], low[head], TN, preferred_element_type=F32)
        vgt[cols, :] = value_t.astype(BF16)
        vg[:, cols] = value_t.T.astype(BF16)
        key_t = scale * lax.dot_general(
            q[0, 0, :, cols], dlow[head], TN, preferred_element_type=F32
        )
        kgt[cols, :] = key_t.astype(BF16)
        kg[:, cols] = key_t.T.astype(BF16)


def attend(queries, cotangent, keys, values):
    _, _, total, width = queries.shape
    span = 4 * keys[0].shape[0]
    same = bf16(*queries.shape)
    return call(
        attend_body,
        [queries, cotangent, *keys, *values],
        [same, same, bf16(span, width), bf16(span, width), bf16(width, span), bf16(width, span)],
        [pltpu.VMEM((width // HEAD_DIM, total, span), BF16)] * 2,
    )


def weight_body(count, offsets, final, index, grad_t, *refs):
    pieces, refs = refs[:count], refs[count:]
    moved, outs = refs[: len(offsets)], refs[len(offsets) :]
    for i in range(index.shape[0]):
        start = pl.multiple_of(index[i] * TILE, TILE)
        rows = jnp.concatenate([piece[:, pl.ds(start, TILE)] for piece in pieces], 0)
        total = jnp.dot(grad_t[...], rows, preferred_element_type=F32)
        for ref, offset in zip(moved, offsets):
            low = (offset + i) * TILE
            total = total + ref[:, low : low + TILE].astype(F32)
        cols = slice(i * TILE, (i + 1) * TILE)
        if final:
            outs[0][cols, :] = total.T.astype(BF16)
        else:
            outs[0][:, cols] = total.astype(BF16)


def weight_part(index, grad_t, pieces, moved=(), offsets=(), final=False):
    span = index.shape[0] * TILE
    width = grad_t.shape[0]
    return call(
        functools.partial(weight_body, len(pieces), offsets, final),
        [index, grad_t, *pieces, *moved],
        bf16(span, width) if final else bf16(width, span),
        index=1,
    )


def encoder_body(low, kg, vg, w, *refs):
    out = refs[-1]
    rows = slice(low, low + out.shape[0])
    for i in range(out.shape[1] // TILE):
        cols = slice(i * TILE, (i + 1) * TILE)
        total = lax.dot_general(kg[rows, :], w[0, 0, cols, :], NT, preferred_element_type=F32)
        total = total + lax.dot_general(
            vg[rows, :], w[0, 1, cols, :], NT, preferred_element_type=F32
        )
        if len(refs) > 1:
            total = total + refs[0][:, cols].astype(F32)
        out[:, cols] = total.astype(BF16)


def encoder_part(key_grad, value_grad, kv_weight, block, *moved):
    rows = key_grad.shape[0] // 4
    return call(
        functools.partial(encoder_body, block * rows),
        [key_grad, value_grad, kv_weight, *moved],
        bf16(rows, kv_weight.shape[2]),
    )


def tie(array, *others):
    return lax.optimization_barrier((array, *others))[0]


def on_device(encoded, kv_weight, queries, cotangent):
    core = lax.axis_index("tensor") % 2
    y = lax.axis_index("dp")
    block = encoded[0]
    half = block.shape[0] // 2

    h = {"o": lax.dynamic_slice_in_dim(block, core * half, half, 0)}
    h_too = {"o": lax.dynamic_slice_in_dim(block, (1 - core) * half, half, 0)}
    g, g_too = {}, {}
    h["a"] = send(h["o"], X_FIRST)
    g["o"] = send(h["o"], ALONG_Z)
    h["b"] = send(tie(h["o"], h["a"]), X_SECOND)
    g["a"] = send(tie(h["a"], g["o"]), ALONG_Z)
    h["d"] = send(tie(h["a"], h["b"]), X_SECOND)
    g["b"] = send(tie(h["b"], g["a"]), ALONG_Z)
    g["d"] = send(tie(h["d"], g["b"]), ALONG_Z)
    for name in "abd":
        h_too[name] = send(h[name], SWAP)
    for name in "oa":
        g_too[name] = send(g[name], SWAP)
    done = [
        project((h["o"], h_too["o"], h["a"], h_too["a"]), kv_weight),
        project((g["o"], g_too["o"], h["b"], h_too["b"]), kv_weight),
        project((g["a"], g_too["a"], h["d"], h_too["d"]), kv_weight),
    ]
    g_too["b"] = send(tie(g["b"], done[0][0], done[1][0]), SWAP)
    g_too["d"] = send(tie(g["d"], done[2][0]), SWAP)
    done.append(project((g["b"], g_too["b"], g["d"], g_too["d"]), kv_weight))
    keys, values = zip(*done)
    order = ["ho", "go", "hb", "gb", "ha", "ga", "hd", "gd"]
    pieces = [{"h": h, "g": g}[name[0]][name[1]] for name in order]
    pieces += [{"h": h_too, "g": g_too}[name[0]][name[1]] for name in order]

    attended, query_grad, key_grad, value_grad, key_grad_t, value_grad_t = attend(
        queries, cotangent, keys, values
    )

    one, other = y ^ 1, 3 - y
    first = jnp.where(core == 0, one, other)
    second = jnp.where(core == 0, other, one)
    across = (y + 2) % 4

    def tiles(*slices):
        return jnp.stack([2 * s + i for s in slices for i in range(2)]).astype(jnp.int32)

    value_out = weight_part(tiles(first, across), value_grad_t, pieces)
    value_in = send(value_out, Y_FIRST)

    key_grad, value_grad = lax.optimization_barrier((key_grad, value_grad, value_out))[:2]
    grads = (key_grad, value_grad, kv_weight)
    moved_send = send(encoder_part(*grads, 3), SWAP)
    moved_keep = send(encoder_part(*grads, 2), SWAP)
    x_out = encoder_part(*grads, 1, moved_send)
    x_in = send(x_out, X_FIRST)

    key_out = weight_part(tiles(first, across), tie(key_grad_t, x_out), pieces)
    key_in = send(tie(key_out, value_in), Y_FIRST)
    keep = encoder_part(tie(key_grad, key_out), value_grad, kv_weight, 0, moved_keep)

    total = keep.astype(F32) + x_in.astype(F32)
    x_in = send(total[2 * half :].astype(BF16), X_SECOND)
    total = total[: 2 * half] + x_in.astype(F32)
    here = total[:half] + send(total[half:].astype(BF16), BACK_Z).astype(F32)
    here = here.astype(BF16)
    last = (here.astype(F32) + send(here, ACROSS_Z).astype(F32)).astype(BF16)
    last_too = send(last, SWAP)
    enc_grad = jnp.where(
        core == 0, jnp.concatenate([last, last_too], 0), jnp.concatenate([last_too, last], 0)
    )

    value_two = weight_part(tiles(second), value_grad_t, pieces, [value_in], [2])
    value_two = send(tie(value_two, key_in), Y_SECOND)
    key_two = weight_part(tiles(second), key_grad_t, pieces, [key_in], [2])
    key_two = send(tie(key_two, value_two), Y_SECOND)
    value_share = weight_part(tiles(y), value_grad_t, pieces, [value_in, value_two], [0, 0], True)
    key_share = weight_part(tiles(y), key_grad_t, pieces, [key_in, key_two], [0, 0], True)
    share = jnp.stack([key_share, value_share], 0)
    return (attended, query_grad, enc_grad[None], share[None])


def solution(mesh):
    return jax.shard_map(
        on_device,
        mesh=mesh,
        in_specs=(
            P("dp", "pipe", None),
            P("pipe", None, None, "tensor"),
            P("dp", "pipe", None, "tensor"),
            P("dp", "pipe", None, "tensor"),
        ),
        out_specs=(
            P("dp", "pipe", None, "tensor"),
            P("dp", "pipe", None, "tensor"),
            P("dp", "pipe", None),
            P("pipe", None, "dp", "tensor"),
        ),
        check_vma=False,
    )
```

time: 531 us -> 184 us (0.35)
  waiting for transfers between devices: 380 us -> 61 us
  matrix products: 66.7 us -> 0 us
  Pallas kernels: 0 us -> 50.6 us
  blocking collectives: 45.4 us -> 0 us
  starting transfers between devices: 0.12 us -> 28.4 us
  local copies, waits for them, and re-layouts: 11.3 us -> 32.7 us
  between operations: 14 us -> 1.24 us
    reduce_scatter x2 -> x0, waiting for transfers between devices: 286 us -> none  [the longest x1 169 us: on_device(): lax.psum_scatter(first + lax.dot_general(value_grad, w_value, cdims, pref...]
    all_gather x1 -> x0, waiting for transfers between devices: 92.7 us -> none  [on_device(): whole = lax.all_gather(encoded, 'pipe', axis=1, tiled=True)[0]]
    dot_general x11 -> x0, matrix products: 63.3 us -> none  [the longest x1 12.8 us: on_device(): lax.dot_general(value_grad, w_value, cdims, preferred_element_type=jnp.fl...]
    ppermute x0 -> x25, waiting for transfers between devices: none -> 61 us  [send(): return lax.ppermute(array, ALL, route)]
    pallas_call x0 -> x15, Pallas kernels: none -> 50.6 us  [call(): pl.pallas_call(body, in_specs=[SCALARS] * index + [WHOLE] * (len(operands...]
    psum x1 -> x0, blocking collectives: 45.4 us -> none  [on_device(): summed = lax.psum(partial_rows, 'tensor')]
    ppermute x0 -> x25, starting transfers between devices: none -> 28.4 us  [send(): return lax.ppermute(array, ALL, route)]
    unnamed x22 -> x108, local copies, waits for them, and re-layouts: 7.87 us -> 30.4 us
  transfers between devices with their start and end apart: 3 -> 25, of which waited for: 3 -> 11; matrix products, arithmetic and copies ran while one was open for 7% -> 3% of each run, Pallas kernels for 0% -> 19%
where the time goes in v2:
time: 184 us; the launch traced here: 181 us
  waiting for transfers between devices  61 us (33%)
  Pallas kernels  50.6 us (28%)
  local copies, waits for them, and re-layouts  32.7 us (18%)
  starting transfers between devices  28.4 us (15%)
  other arithmetic  7.44 us (4%)
    ppermute x25, waiting for transfers between devices, send(): return lax.ppermute(array, ALL, route)  61 us
    pallas_call x15, Pallas kernels, call(): pl.pallas_call(body, in_specs=[SCALARS] * index + [WHOLE] * (len(operands...  50.6 us
    unnamed x108, local copies, waits for them, and re-layouts  30.4 us
    ppermute x25, starting transfers between devices, send(): return lax.ppermute(array, ALL, route)  28.4 us
  transfers between devices with their start and end apart: 25, of which 11 were waited for; matrix products, arithmetic and copies ran while one was open for 3% of the time, Pallas kernels for 19%

profile of v2, /device:TPU:0, one launch (start us, length us, event | category | flops | bytes accessed | tf_op | source)
XLA Modules:
  0.0 181.3 jit_solution(5396784048000506734)
XLA Ops:
  0.7 1.3 dynamic-slice_bitcast_fusion
  1.9 1.7 collective-permute-start
  3.6 1.9 %collective-permute-start.2 = (bf16[64,4096]{1,0:T(8,128)(2,1)S(1)}, bf16[64,4096]{1,0:T(8,128)(2,1)S(1)}, u32[]{:S(2)}, u32[]{:S(2)}) collective-permute-start(bf16[64,4096]{1,0:T(8,128)(2,1)S(1)} %get-tuple-element.33.a.refs_0_), channel_id=1, source_target_pairs={{0,64},{4,76},{64,8},{68,4},{8,72},{12,68},{72,0},{76,12},{1,65},{... | collective-permute-start | bytes 1572872 | tf_op jit(solution)/shard_map/ppermute | solution.py:68
  5.5 5.7 %collective-permute-done.c.refs_4_ = bf16[64,4096]{1,0:T(8,128)(2,1)S(1)} collective-permute-done((bf16[64,4096]{1,0:T(8,128)(2,1)S(1)}, bf16[64,4096]{1,0:T(8,128)(2,1)S(1)}, u32[]{:S(2)}, u32[]{:S(2)}) %collective-permute-start) | collective-permute-done | bytes 524320 | tf_op jit(solution)/shard_map/ppermute | solution.py:68
  11.2 2.8 %collective-permute-start.4 = (bf16[64,4096]{1,0:T(8,128)(2,1)S(1)}, bf16[64,4096]{1,0:T(8,128)(2,1)S(1)}, u32[]{:S(2)}, u32[]{:S(2)}) collective-permute-start(bf16[64,4096]{1,0:T(8,128)(2,1)S(1)} %get-tuple-element.33.a.refs_0_), channel_id=1, source_target_pairs={{0,48},{4,20},{64,112},{68,84},{8,56},{12,28},{72,120},{76,92},{1,... | collective-permute-start | bytes 1572872 | tf_op jit(solution)/shard_map/ppermute | solution.py:68
  14.8 1.2 collective-permute-start.6
  16.0 5.6 %collective-permute-done.4.c.refs_2_ = bf16[64,4096]{1,0:T(8,128)(2,1)S(1)} collective-permute-done((bf16[64,4096]{1,0:T(8,128)(2,1)S(1)}, bf16[64,4096]{1,0:T(8,128)(2,1)S(1)}, u32[]{:S(2)}, u32[]{:S(2)}) %collective-permute-start.4) | collective-permute-done | bytes 524320 | tf_op jit(solution)/shard_map/ppermute | solution.py:68
  21.6 2.8 %collective-permute-start.8 = (bf16[64,4096]{1,0:T(8,128)(2,1)S(1)}, bf16[64,4096]{1,0:T(8,128)(2,1)S(1)}, u32[]{:S(2)}, u32[]{:S(2)}) collective-permute-start(bf16[64,4096]{1,0:T(8,128)(2,1)S(1)} %collective-permute-done.c.refs_4_), channel_id=1, source_target_pairs={{0,48},{4,20},{64,112},{68,84},{8,56},{12,28},{72,120},{76,92},{1,... | collective-permute-start | bytes 1572872 | tf_op jit(solution)/shard_map/ppermute | solution.py:68
  25.2 1.1 collective-permute-start.10
  27.2 4.8 %collective-permute-done.8.c.refs_6_ = bf16[64,4096]{1,0:T(8,128)(2,1)S(1)} collective-permute-done((bf16[64,4096]{1,0:T(8,128)(2,1)S(1)}, bf16[64,4096]{1,0:T(8,128)(2,1)S(1)}, u32[]{:S(2)}, u32[]{:S(2)}) %collective-permute-start.8) | collective-permute-done | bytes 524320 | tf_op jit(solution)/shard_map/ppermute | solution.py:68
  32.0 3.7 %collective-permute-done.10.a.refs_3_ = bf16[64,4096]{1,0:T(8,128)(2,1)} collective-permute-done((bf16[64,4096]{1,0:T(8,128)(2,1)S(1)}, bf16[64,4096]{1,0:T(8,128)(2,1)}, u32[]{:S(2)}, u32[]{:S(2)}) %collective-permute-start.10) | collective-permute-done | bytes 524320 | tf_op jit(solution)/shard_map/ppermute | solution.py:68
  35.8 3.5 %copy-done = bf16[1,2,4096,512]{3,2,1,0:T(8,128)(2,1)S(1)} copy-done((bf16[1,2,4096,512]{3,2,1,0:T(8,128)(2,1)S(1)}, bf16[1,2,4096,512]{3,2,1,0:T(8,128)(2,1)}, u32[]{:S(2)}) %copy-start) | copy-done | bytes 8388632
  39.3 2.3 %shard_map.75 = (bf16[256,512]{1,0:T(8,128)(2,1)S(1)}, bf16[256,512]{1,0:T(8,128)(2,1)S(1)}) custom-call(bf16[64,4096]{1,0:T(8,128)(2,1)S(1)} %get-tuple-element.33.a.refs_0_, bf16[64,4096]{1,0:T(8,128)(2,1)S(1)} %get-tuple-element.60.b.refs_8_, bf16[64,4096]{1,0:T(8,128)(2,1)S(1)} %collective-permute-done.c.refs_4_, ...), custom_call_target="tpu_custom_call" | custom-call | flops 1000 | bytes 1000 | tf_op jit(solution)/shard_map/pallas_call | solution.py:22
  42.8 2.3 %shard_map.76 = (bf16[256,512]{1,0:T(8,128)(2,1)S(1)}, bf16[256,512]{1,0:T(8,128)(2,1)S(1)}) custom-call(bf16[64,4096]{1,0:T(8,128)(2,1)S(1)} %collective-permute-done.2.a.refs_1_, bf16[64,4096]{1,0:T(8,128)(2,1)S(1)} %collective-permute-done.3.b.refs_9_, bf16[64,4096]{1,0:T(8,128)(2,1)S(1)} %collective-permute-done.4.c.refs_2_, ...), custom_call_target="tpu_custom_call" | custom-call | flops 1000 | bytes 1000 | tf_op jit(solution)/shard_map/pallas_call | solution.py:22
  45.1 2.1 %collective-permute-start.11 = (bf16[64,4096]{1,0:T(8,128)(2,1)}, bf16[64,4096]{1,0:T(8,128)(2,1)}, u32[]{:S(2)}, u32[]{:S(2)}) collective-permute-start(bf16[64,4096]{1,0:T(8,128)(2,1)} %collective-permute-done.10.a.refs_3_), channel_id=1, source_target_pairs={{0,4},{4,0},{64,68},{68,64},{8,12},{12,8},{72,76},{76,72},{1,5},{5... | collective-permute-start | bytes 1572872 | tf_op jit(solution)/shard_map/ppermute | solution.py:68
  47.3 2.3 %shard_map.77 = (bf16[256,512]{1,0:T(8,128)(2,1)S(1)}, bf16[256,512]{1,0:T(8,128)(2,1)S(1)}) custom-call(bf16[64,4096]{1,0:T(8,128)(2,1)S(1)} %collective-permute-done.6.a.refs_5_, bf16[64,4096]{1,0:T(8,128)(2,1)S(1)} %collective-permute-done.7.b.refs_13_, bf16[64,4096]{1,0:T(8,128)(2,1)S(1)} %collective-permute-done.8.c.refs_6_, ...), custom_call_target="tpu_custom_call" | custom-call | flops 1000 | bytes 1000 | tf_op jit(solution)/shard_map/pallas_call | solution.py:22
  51.2 2.1 %collective-permute-done.13.d.refs_15_ = bf16[64,4096]{1,0:T(8,128)(2,1)} collective-permute-done((bf16[64,4096]{1,0:T(8,128)(2,1)}, bf16[64,4096]{1,0:T(8,128)(2,1)}, u32[]{:S(2)}, u32[]{:S(2)}) %collective-permute-start.13) | collective-permute-done | bytes 524320 | tf_op jit(solution)/shard_map/ppermute | solution.py:68
  53.3 3.4 %copy-done.2 = bf16[1,2,4096,512]{3,2,1,0:T(8,128)(2,1)S(1)} copy-done((bf16[1,2,4096,512]{3,2,1,0:T(8,128)(2,1)S(1)}, bf16[1,2,4096,512]{3,2,1,0:T(8,128)(2,1)}, u32[]{:S(2)}) %copy-start.2) | copy-done | bytes 8388632
  56.8 4.0 %shard_map.78 = (bf16[256,512]{1,0:T(8,128)(2,1)S(1)}, bf16[256,512]{1,0:T(8,128)(2,1)S(1)}) custom-call(bf16[64,4096]{1,0:T(8,128)(2,1)} %collective-permute-done.10.a.refs_3_, bf16[64,4096]{1,0:T(8,128)(2,1)} %collective-permute-done.11.b.refs_11_, bf16[64,4096]{1,0:T(8,128)(2,1)} %collective-permute-done.12.c.refs_7_, ...), custom_call_target="tpu_custom_call" | custom-call | flops 1000 | bytes 1000 | tf_op jit(solution)/shard_map/pallas_call | solution.py:22
  60.9 6.0 %shard_map.79 = (bf16[1,1,512,512]{3,2,1,0:T(8,128)(2,1)}, bf16[1,1,512,512]{3,2,1,0:T(8,128)(2,1)}, bf16[1024,512]{1,0:T(8,128)(2,1)S(1)}, bf16[1024,512]{1,0:T...) custom-call(bf16[1,1,512,512]{3,2,1,0:T(8,128)(2,1)S(1)} %copy-done.38, ...), custom_call_target="tpu_custom_call" | custom-call | flops 1000 | bytes 1000 | tf_op jit(solution)/shard_map/pallas_call | solution.py:22
  66.9 4.6 %shard_map.80 = bf16[512,2048]{1,0:T(8,128)(2,1)S(1)} custom-call(s32[4]{0:T(128)S(1)} %pad_add_fusion.index, bf16[512,1024]{1,0:T(8,128)(2,1)S(1)} %get-tuple-element.51.grad_t, bf16[64,4096]{1,0:T(8,128)(2,1)S(1)} %get-tuple-element.33.a.refs_0_, bf16[64,4096]{1,0:T(8,128)(2,1)S(1)} %collective-permute-done.2.a.refs_1_, ...), custom_call_target="tpu_custom_call" | custom-call | flops 1000 | bytes 1000 | tf_op jit(solution)/shard_map/pallas_call | solution.py:22
  71.6 2.4 %shard_map.81 = bf16[256,4096]{1,0:T(8,128)(2,1)S(1)} custom-call(bf16[1024,512]{1,0:T(8,128)(2,1)S(1)} %get-tuple-element.56.kg, bf16[1024,512]{1,0:T(8,128)(2,1)S(1)} %get-tuple-element.54.vg, bf16[1,2,4096,512]{3,2,1,0:T(8,128)(2,1)S(1)} %bitcast.19), custom_call_target="tpu_custom_call" | custom-call | flops 1000 | bytes 1000 | tf_op jit(solution)/shard_map/pallas_call | solution.py:22
  74.2 2.4 %shard_map.84 = bf16[256,4096]{1,0:T(8,128)(2,1)S(1)} custom-call(bf16[1024,512]{1,0:T(8,128)(2,1)S(1)} %get-tuple-element.56.kg, bf16[1024,512]{1,0:T(8,128)(2,1)S(1)} %get-tuple-element.54.vg, bf16[1,2,4096,512]{3,2,1,0:T(8,128)(2,1)S(1)} %bitcast.19), custom_call_target="tpu_custom_call" | custom-call | flops 1000 | bytes 1000 | tf_op jit(solution)/shard_map/pallas_call | solution.py:22
  78.2 2.4 %shard_map.82 = bf16[256,4096]{1,0:T(8,128)(2,1)S(1)} custom-call(bf16[1024,512]{1,0:T(8,128)(2,1)S(1)} %get-tuple-element.56.kg, bf16[1024,512]{1,0:T(8,128)(2,1)S(1)} %get-tuple-element.54.vg, bf16[1,2,4096,512]{3,2,1,0:T(8,128)(2,1)S(1)} %bitcast.19, bf16[256,4096]{1,0:T(8,128)(2,1)S(1)} %collective-permute-done.14.refs_0_), custom_call_target="tpu_custom_call" | custom-call | flops 1000 | bytes 1000 | tf_op jit(solution)/shard_map/pallas_call | solution.py:22
  80.7 1.7 collective-permute-start.21
  82.3 5.2 %shard_map.83 = bf16[512,2048]{1,0:T(8,128)(2,1)} custom-call(s32[4]{0:T(128)S(1)} %pad_add_fusion.index, bf16[512,1024]{1,0:T(8,128)(2,1)S(1)} %get-tuple-element.55.grad_t, bf16[64,4096]{1,0:T(8,128)(2,1)S(1)} %get-tuple-element.33.a.refs_0_, bf16[64,4096]{1,0:T(8,128)(2,1)S(1)} %collective-permute-done.2.a.refs_1_, ...), custom_call_target="tpu_custom_call" | custom-call | flops 1000 | bytes 1000 | tf_op jit(solution)/shard_map/pallas_call | solution.py:22
  87.6 2.4 %shard_map.85 = bf16[256,4096]{1,0:T(8,128)(2,1)S(1)} custom-call(bf16[1024,512]{1,0:T(8,128)(2,1)S(1)} %get-tuple-element.56.kg, bf16[1024,512]{1,0:T(8,128)(2,1)S(1)} %get-tuple-element.54.vg, bf16[1,2,4096,512]{3,2,1,0:T(8,128)(2,1)S(1)} %bitcast.19, bf16[256,4096]{1,0:T(8,128)(2,1)S(1)} %collective-permute-done.15.refs_0_), custom_call_target="tpu_custom_call" | custom-call | flops 1000 | bytes 1000 | tf_op jit(solution)/shard_map/pallas_call | solution.py:22
  89.9 16.7 %collective-permute-done.16 = bf16[256,4096]{1,0:T(8,128)(2,1)S(1)} collective-permute-done((bf16[256,4096]{1,0:T(8,128)(2,1)S(1)}, bf16[256,4096]{1,0:T(8,128)(2,1)S(1)}, u32[]{:S(2)}, u32[]{:S(2)}) %collective-permute-start.16) | collective-permute-done | bytes 2097184 | tf_op jit(solution)/shard_map/ppermute | solution.py:68
  107.5 1.3 collective-permute-start.17
  108.8 1.6 collective-permute-start.22
  110.4 13.2 %collective-permute-done.17 = bf16[128,4096]{1,0:T(8,128)(2,1)S(1)} collective-permute-done((bf16[128,4096]{1,0:T(8,128)(2,1)S(1)}, bf16[128,4096]{1,0:T(8,128)(2,1)S(1)}, u32[]{:S(2)}, u32[]{:S(2)}) %collective-permute-start.17) | collective-permute-done | bytes 1048608 | tf_op jit(solution)/shard_map/ppermute | solution.py:68
  125.3 1.2 collective-permute-start.18
  132.9 1.2 copy-done.31
  134.1 1.6 copy-done.34
  135.7 2.9 %shard_map.87 = bf16[512,1024]{1,0:T(8,128)(2,1)S(1)} custom-call(s32[2]{0:T(128)S(1)} %pad_add_fusion.2.index, bf16[512,1024]{1,0:T(8,128)(2,1)S(1)} %copy-done.31, bf16[64,4096]{1,0:T(8,128)(2,1)S(1)} %get-tuple-element.33.a.refs_0_, bf16[64,4096]{1,0:T(8,128)(2,1)S(1)} %collective-permute-done.2.a.refs_1_, ...), custom_call_target="tpu_custom_call" | custom-call | flops 1000 | bytes 1000 | tf_op jit(solution)/shard_map/pallas_call | solution.py:22
  138.6 3.1 %collective-permute-start.23 = (bf16[512,1024]{1,0:T(8,128)(2,1)S(1)}, bf16[512,1024]{1,0:T(8,128)(2,1)S(1)}, u32[]{:S(2)}, u32[]{:S(2)}) collective-permute-start(bf16[512,1024]{1,0:T(8,128)(2,1)S(1)} %shard_map.87), channel_id=1, source_target_pairs={{0,3},{4,5},{64,67},{68,69},{8,11},{12,13},{72,75},{76,77},{1,2},{... | collective-permute-start | bytes 3145736 | tf_op jit(solution)/shard_map/ppermute | solution.py:68
  141.7 1.1 fusion
  143.8 4.5 %shard_map.86 = bf16[512,1024]{1,0:T(8,128)(2,1)} custom-call(s32[2]{0:T(128)S(1)} %pad_add_fusion.2.index, bf16[512,1024]{1,0:T(8,128)(2,1)S(1)} %copy-done.28, bf16[64,4096]{1,0:T(8,128)(2,1)S(1)} %get-tuple-element.33.a.refs_0_, bf16[64,4096]{1,0:T(8,128)(2,1)S(1)} %collective-permute-done.2.a.refs_1_, ...), custom_call_target="tpu_custom_call" | custom-call | flops 1000 | bytes 1000 | tf_op jit(solution)/shard_map/pallas_call | solution.py:22
  148.3 6.4 %collective-permute-done.23.refs_17_ = bf16[512,1024]{1,0:T(8,128)(2,1)S(1)} collective-permute-done((bf16[512,1024]{1,0:T(8,128)(2,1)S(1)}, bf16[512,1024]{1,0:T(8,128)(2,1)S(1)}, u32[]{:S(2)}, u32[]{:S(2)}) %collective-permute-start.23) | collective-permute-done | bytes 1048608 | tf_op jit(solution)/shard_map/ppermute | solution.py:68
  155.7 3.0 %collective-permute-start.24 = (bf16[512,1024]{1,0:T(8,128)(2,1)}, bf16[512,1024]{1,0:T(8,128)(2,1)}, u32[]{:S(2)}, u32[]{:S(2)}) collective-permute-start(bf16[512,1024]{1,0:T(8,128)(2,1)} %shard_map.86), channel_id=1, source_target_pairs={{0,3},{4,5},{64,67},{68,69},{8,11},{12,13},{72,75},{76,77},{1,2},{... | collective-permute-start | bytes 3145736 | tf_op jit(solution)/shard_map/ppermute | solution.py:68
  159.7 1.0 copy-done.6
  166.0 1.2 copy-done.32
  167.2 1.6 copy-done.35
  168.8 1.2 copy-done.37
  170.0 3.0 %shard_map.89 = bf16[1024,512]{1,0:T(8,128)(2,1)S(1)} custom-call(s32[2]{0:T(128)S(1)} %pad_add_fusion.1.index, bf16[512,1024]{1,0:T(8,128)(2,1)S(1)} %copy-done.32, bf16[64,4096]{1,0:T(8,128)(2,1)S(1)} %get-tuple-element.33.a.refs_0_, bf16[64,4096]{1,0:T(8,128)(2,1)S(1)} %collective-permute-done.2.a.refs_1_, ...), custom_call_target="tpu_custom_call" | custom-call | flops 1000 | bytes 1000 | tf_op jit(solution)/shard_map/pallas_call | solution.py:22
  173.1 3.9 %shard_map.88 = bf16[1024,512]{1,0:T(8,128)(2,1)S(1)} custom-call(s32[2]{0:T(128)S(1)} %pad_add_fusion.1.index, bf16[512,1024]{1,0:T(8,128)(2,1)S(1)} %copy-done.29, bf16[64,4096]{1,0:T(8,128)(2,1)S(1)} %get-tuple-element.33.a.refs_0_, bf16[64,4096]{1,0:T(8,128)(2,1)S(1)} %collective-permute-done.2.a.refs_1_, ...), custom_call_target="tpu_custom_call" | custom-call | flops 1000 | bytes 1000 | tf_op jit(solution)/shard_map/pallas_call | solution.py:22
  177.0 1.5 maximum_bitcast_fusion
  178.5 2.7 %maximum_select_fusion = bf16[1,128,4096]{2,1,0:T(8,128)(2,1)} fusion(bf16[1,64,4096]{2,1,0:T(8,128)(2,1)} %bitcast.7, bf16[1,64,4096]{2,1,0:T(8,128)(2,1)} %bitcast.6, pred[]{:T(512)S(6)} %eq.8), kind=kLoop, calls=%fused_computation.7 | loop fusion | flops 4718592 | bytes 2097153 | tf_op jit(solution)/shard_map/jit(_where)/select_n | solution.py:264
  (138 shorter events, 24.1 us)
Async XLA Ops:
  1.9 9.3 %collective-permute-start = (bf16[64,4096]{1,0:T(8,128)(2,1)S(1)}, bf16[64,4096]{1,0:T(8,128)(2,1)S(1)}, u32[]{:S(2)}, u32[]{:S(2)}) collective-permute-start(bf16[64,4096]{1,0:T(8,128)(2,1)S(1)} %get-tuple-element.33.a.refs_0_), channel_id=1, source_target_pairs={{0,16},{4,52},{64,80},{68,116},{8,24},{12,60},{72,88},{76,124},{1,... | collective-permute-start | bytes 1572872 | tf_op jit(solution)/shard_map/ppermute | solution.py:68
  3.6 11.2 %collective-permute-start.2 = (bf16[64,4096]{1,0:T(8,128)(2,1)S(1)}, bf16[64,4096]{1,0:T(8,128)(2,1)S(1)}, u32[]{:S(2)}, u32[]{:S(2)}) collective-permute-start(bf16[64,4096]{1,0:T(8,128)(2,1)S(1)} %get-tuple-element.33.a.refs_0_), channel_id=1, source_target_pairs={{0,64},{4,76},{64,8},{68,4},{8,72},{12,68},{72,0},{76,12},{1,65},{... | collective-permute-start | bytes 1572872 | tf_op jit(solution)/shard_map/ppermute | solution.py:68
  11.2 10.4 %collective-permute-start.4 = (bf16[64,4096]{1,0:T(8,128)(2,1)S(1)}, bf16[64,4096]{1,0:T(8,128)(2,1)S(1)}, u32[]{:S(2)}, u32[]{:S(2)}) collective-permute-start(bf16[64,4096]{1,0:T(8,128)(2,1)S(1)} %get-tuple-element.33.a.refs_0_), channel_id=1, source_target_pairs={{0,48},{4,20},{64,112},{68,84},{8,56},{12,28},{72,120},{76,92},{1,... | collective-permute-start | bytes 1572872 | tf_op jit(solution)/shard_map/ppermute | solution.py:68
  14.8 10.5 %collective-permute-start.6 = (bf16[64,4096]{1,0:T(8,128)(2,1)S(1)}, bf16[64,4096]{1,0:T(8,128)(2,1)S(1)}, u32[]{:S(2)}, u32[]{:S(2)}) collective-permute-start(bf16[64,4096]{1,0:T(8,128)(2,1)S(1)} %collective-permute-done.c.refs_4_), channel_id=1, source_target_pairs={{0,64},{4,76},{64,8},{68,4},{8,72},{12,68},{72,0},{76,12},{1,65},{... | collective-permute-start | bytes 1572872 | tf_op jit(solution)/shard_map/ppermute | solution.py:68
  21.6 10.4 %collective-permute-start.8 = (bf16[64,4096]{1,0:T(8,128)(2,1)S(1)}, bf16[64,4096]{1,0:T(8,128)(2,1)S(1)}, u32[]{:S(2)}, u32[]{:S(2)}) collective-permute-start(bf16[64,4096]{1,0:T(8,128)(2,1)S(1)} %collective-permute-done.c.refs_4_), channel_id=1, source_target_pairs={{0,48},{4,20},{64,112},{68,84},{8,56},{12,28},{72,120},{76,92},{1,... | collective-permute-start | bytes 1572872 | tf_op jit(solution)/shard_map/ppermute | solution.py:68
  25.2 10.5 %collective-permute-start.10 = (bf16[64,4096]{1,0:T(8,128)(2,1)S(1)}, bf16[64,4096]{1,0:T(8,128)(2,1)}, u32[]{:S(2)}, u32[]{:S(2)}) collective-permute-start(bf16[64,4096]{1,0:T(8,128)(2,1)S(1)} %collective-permute-done.4.c.refs_2_), channel_id=1, source_target_pairs={{0,64},{4,76},{64,8},{68,4},{8,72},{12,68},{72,0},{76,12},{1,65},{... | collective-permute-start | bytes 1572872 | tf_op jit(solution)/shard_map/ppermute | solution.py:68
  26.3 9.4 %collective-permute-start.1 = (bf16[64,4096]{1,0:T(8,128)(2,1)S(1)}, bf16[64,4096]{1,0:T(8,128)(2,1)S(1)}, u32[]{:S(2)}, u32[]{:S(2)}) collective-permute-start(bf16[64,4096]{1,0:T(8,128)(2,1)S(1)} %collective-permute-done.c.refs_4_), channel_id=1, source_target_pairs={{0,4},{4,0},{64,68},{68,64},{8,12},{12,8},{72,76},{76,72},{1,5},{5... | collective-permute-start | bytes 1572872 | tf_op jit(solution)/shard_map/ppermute | solution.py:68
  26.6 15.7 %collective-permute-start.3 = (bf16[64,4096]{1,0:T(8,128)(2,1)S(1)}, bf16[64,4096]{1,0:T(8,128)(2,1)S(1)}, u32[]{:S(2)}, u32[]{:S(2)}) collective-permute-start(bf16[64,4096]{1,0:T(8,128)(2,1)S(1)} %collective-permute-done.2.a.refs_1_), channel_id=1, source_target_pairs={{0,4},{4,0},{64,68},{68,64},{8,12},{12,8},{72,76},{76,72},{1,5},{5... | collective-permute-start | bytes 1572872 | tf_op jit(solution)/shard_map/ppermute | solution.py:68
  26.9 15.5 %collective-permute-start.5 = (bf16[64,4096]{1,0:T(8,128)(2,1)S(1)}, bf16[64,4096]{1,0:T(8,128)(2,1)S(1)}, u32[]{:S(2)}, u32[]{:S(2)}) collective-permute-start(bf16[64,4096]{1,0:T(8,128)(2,1)S(1)} %collective-permute-done.4.c.refs_2_), channel_id=1, source_target_pairs={{0,4},{4,0},{64,68},{68,64},{8,12},{12,8},{72,76},{76,72},{1,5},{5... | collective-permute-start | bytes 1572872 | tf_op jit(solution)/shard_map/ppermute | solution.py:68
  32.0 15.3 %copy-start.3 = (bf16[64,4096]{1,0:T(8,128)(2,1)}, bf16[64,4096]{1,0:T(8,128)(2,1)S(1)}, u32[]{:S(2)}) copy-start(bf16[64,4096]{1,0:T(8,128)(2,1)S(1)} %collective-permute-done.8.c.refs_6_) | copy-start | bytes 1572868
  32.0 15.3 %collective-permute-start.7 = (bf16[64,4096]{1,0:T(8,128)(2,1)S(1)}, bf16[64,4096]{1,0:T(8,128)(2,1)S(1)}, u32[]{:S(2)}, u32[]{:S(2)}) collective-permute-start(bf16[64,4096]{1,0:T(8,128)(2,1)S(1)} %collective-permute-done.6.a.refs_5_), channel_id=1, source_target_pairs={{0,4},{4,0},{64,68},{68,64},{8,12},{12,8},{72,76},{76,72},{1,5},{5... | collective-permute-start | bytes 1572872 | tf_op jit(solution)/shard_map/ppermute | solution.py:68
  35.7 11.6 %collective-permute-start.9 = (bf16[64,4096]{1,0:T(8,128)(2,1)S(1)}, bf16[64,4096]{1,0:T(8,128)(2,1)S(1)}, u32[]{:S(2)}, u32[]{:S(2)}) collective-permute-start(bf16[64,4096]{1,0:T(8,128)(2,1)S(1)} %collective-permute-done.8.c.refs_6_), channel_id=1, source_target_pairs={{0,4},{4,0},{64,68},{68,64},{8,12},{12,8},{72,76},{76,72},{1,5},{5... | collective-permute-start | bytes 1572872 | tf_op jit(solution)/shard_map/ppermute | solution.py:68
  35.7 5.9 %copy-start.7 = (bf16[64,4096]{1,0:T(8,128)(2,1)}, bf16[64,4096]{1,0:T(8,128)(2,1)S(1)}, u32[]{:S(2)}) copy-start(bf16[64,4096]{1,0:T(8,128)(2,1)S(1)} %collective-permute-done.1.d.refs_12_) | copy-start | bytes 1572868
  35.7 15.3 %collective-permute-start.12 = (bf16[64,4096]{1,0:T(8,128)(2,1)S(1)}, bf16[64,4096]{1,0:T(8,128)(2,1)}, u32[]{:S(2)}, u32[]{:S(2)}) collective-permute-start(bf16[64,4096]{1,0:T(8,128)(2,1)S(1)} %collective-permute-done.8.c.refs_6_), channel_id=1, source_target_pairs={{0,64},{4,76},{64,8},{68,4},{8,72},{12,68},{72,0},{76,12},{1,65},{... | collective-permute-start | bytes 1572872 | tf_op jit(solution)/shard_map/ppermute | solution.py:68
  45.1 4.5 %copy-start.42 = (bf16[256,512]{1,0:T(8,128)(2,1)}, bf16[256,512]{1,0:T(8,128)(2,1)S(1)}, u32[]{:S(2)}) copy-start(bf16[256,512]{1,0:T(8,128)(2,1)S(1)} %get-tuple-element.34.k1) | copy-start | bytes 786436
  45.1 4.5 %copy-start.44 = (bf16[256,512]{1,0:T(8,128)(2,1)}, bf16[256,512]{1,0:T(8,128)(2,1)S(1)}, u32[]{:S(2)}) copy-start(bf16[256,512]{1,0:T(8,128)(2,1)S(1)} %get-tuple-element.44.v1) | copy-start | bytes 786436
  45.1 6.0 %collective-permute-start.11 = (bf16[64,4096]{1,0:T(8,128)(2,1)}, bf16[64,4096]{1,0:T(8,128)(2,1)}, u32[]{:S(2)}, u32[]{:S(2)}) collective-permute-start(bf16[64,4096]{1,0:T(8,128)(2,1)} %collective-permute-done.10.a.refs_3_), channel_id=1, source_target_pairs={{0,4},{4,0},{64,68},{68,64},{8,12},{12,8},{72,76},{76,72},{1,5},{5... | collective-permute-start | bytes 1572872 | tf_op jit(solution)/shard_map/ppermute | solution.py:68
  51.1 2.3 %collective-permute-start.13 = (bf16[64,4096]{1,0:T(8,128)(2,1)}, bf16[64,4096]{1,0:T(8,128)(2,1)}, u32[]{:S(2)}, u32[]{:S(2)}) collective-permute-start(bf16[64,4096]{1,0:T(8,128)(2,1)} %collective-permute-done.12.c.refs_7_), channel_id=1, source_target_pairs={{0,4},{4,0},{64,68},{68,64},{8,12},{12,8},{72,76},{76,72},{1,5},{5... | collective-permute-start | bytes 1572872 | tf_op jit(solution)/shard_map/ppermute | solution.py:68
  56.7 4.1 %copy-start.39 = (bf16[1,1,512,512]{3,2,1,0:T(8,128)(2,1)S(1)}, bf16[1,1,512,512]{3,2,1,0:T(8,128)(2,1)}, u32[]{:S(2)}) copy-start(bf16[1,1,512,512]{3,2,1,0:T(8,128)(2,1)} %g.1) | copy-start | bytes 1572868
  56.7 4.1 %copy-start.41 = (bf16[256,512]{1,0:T(8,128)(2,1)S(1)}, bf16[256,512]{1,0:T(8,128)(2,1)}, u32[]{:S(2)}) copy-start(bf16[256,512]{1,0:T(8,128)(2,1)} %copy-done.40) | copy-start | bytes 786436
  56.7 4.1 %copy-start.43 = (bf16[256,512]{1,0:T(8,128)(2,1)S(1)}, bf16[256,512]{1,0:T(8,128)(2,1)}, u32[]{:S(2)}) copy-start(bf16[256,512]{1,0:T(8,128)(2,1)} %copy-done.42) | copy-start | bytes 786436
  56.7 4.1 %copy-start.45 = (bf16[256,512]{1,0:T(8,128)(2,1)S(1)}, bf16[256,512]{1,0:T(8,128)(2,1)}, u32[]{:S(2)}) copy-start(bf16[256,512]{1,0:T(8,128)(2,1)} %copy-done.44) | copy-start | bytes 786436
  56.7 4.1 %copy-start.47 = (bf16[256,512]{1,0:T(8,128)(2,1)S(1)}, bf16[256,512]{1,0:T(8,128)(2,1)}, u32[]{:S(2)}) copy-start(bf16[256,512]{1,0:T(8,128)(2,1)} %copy-done.46) | copy-start | bytes 786436
  56.8 4.1 %copy-start.49 = (bf16[256,512]{1,0:T(8,128)(2,1)S(1)}, bf16[256,512]{1,0:T(8,128)(2,1)}, u32[]{:S(2)}) copy-start(bf16[256,512]{1,0:T(8,128)(2,1)} %copy-done.48) | copy-start | bytes 786436
  56.8 14.8 %slice-start = ((s8[8388608]{0:T(1024)(128)(4,1)}), s8[4194304]{0:T(1024)(128)(4,1)S(1)}, s32[]{:S(2)}) async-start(s8[8388608]{0:T(1024)(128)(4,1)} %bitcast.18), calls=%async_computation | async-start | bytes 8388608
  60.8 6.1 %copy-start.4 = (bf16[64,4096]{1,0:T(8,128)(2,1)S(1)}, bf16[64,4096]{1,0:T(8,128)(2,1)}, u32[]{:S(2)}) copy-start(bf16[64,4096]{1,0:T(8,128)(2,1)} %copy-done.3) | copy-start | bytes 1572868
  60.8 6.1 %copy-start.8 = (bf16[64,4096]{1,0:T(8,128)(2,1)S(1)}, bf16[64,4096]{1,0:T(8,128)(2,1)}, u32[]{:S(2)}) copy-start(bf16[64,4096]{1,0:T(8,128)(2,1)} %copy-done.7) | copy-start | bytes 1572868
  60.8 6.1 %copy-start.12 = (bf16[64,4096]{1,0:T(8,128)(2,1)S(1)}, bf16[64,4096]{1,0:T(8,128)(2,1)}, u32[]{:S(2)}) copy-start(bf16[64,4096]{1,0:T(8,128)(2,1)} %copy-done.11) | copy-start | bytes 1572868
  60.8 6.1 %copy-start.16 = (bf16[64,4096]{1,0:T(8,128)(2,1)S(1)}, bf16[64,4096]{1,0:T(8,128)(2,1)}, u32[]{:S(2)}) copy-start(bf16[64,4096]{1,0:T(8,128)(2,1)} %copy-done.15) | copy-start | bytes 1572868
  60.8 6.1 %copy-start.20 = (bf16[64,4096]{1,0:T(8,128)(2,1)S(1)}, bf16[64,4096]{1,0:T(8,128)(2,1)}, u32[]{:S(2)}) copy-start(bf16[64,4096]{1,0:T(8,128)(2,1)} %copy-done.19) | copy-start | bytes 1572868
  60.8 6.1 %copy-start.24 = (bf16[64,4096]{1,0:T(8,128)(2,1)S(1)}, bf16[64,4096]{1,0:T(8,128)(2,1)}, u32[]{:S(2)}) copy-start(bf16[64,4096]{1,0:T(8,128)(2,1)} %copy-done.23) | copy-start | bytes 1572868
  60.9 10.7 %slice-start.1 = ((s8[8388608]{0:T(1024)(128)(4,1)}), s8[4194304]{0:T(1024)(128)(4,1)S(1)}, s32[]{:S(2)}) async-start(s8[8388608]{0:T(1024)(128)(4,1)} %bitcast.18), calls=%async_computation.1 | async-start | bytes 8388608
  66.9 4.7 %copy-start.30 = (bf16[512,1024]{1,0:T(8,128)(2,1)}, bf16[512,1024]{1,0:T(8,128)(2,1)S(1)}, u32[]{:S(2)}) copy-start(bf16[512,1024]{1,0:T(8,128)(2,1)S(1)} %get-tuple-element.51.grad_t) | copy-start | bytes 3145732
  66.9 15.4 %copy-start.27 = (bf16[512,1024]{1,0:T(8,128)(2,1)}, bf16[512,1024]{1,0:T(8,128)(2,1)S(1)}, u32[]{:S(2)}) copy-start(bf16[512,1024]{1,0:T(8,128)(2,1)S(1)} %get-tuple-element.55.grad_t) | copy-start | bytes 3145732
  73.9 4.2 %collective-permute-start.14 = (bf16[256,4096]{1,0:T(8,128)(2,1)S(1)}, bf16[256,4096]{1,0:T(8,128)(2,1)S(1)}, u32[]{:S(2)}, u32[]{:S(2)}) collective-permute-start(bf16[256,4096]{1,0:T(8,128)(2,1)S(1)} %shard_map.81), channel_id=1, source_target_pairs={{0,4},{4,0},{64,68},{68,64},{8,12},{12,8},{72,76},{76,72},{1,5},{5... | collective-permute-start | bytes 6291464 | tf_op jit(solution)/shard_map/ppermute | solution.py:68
  76.5 11.0 %collective-permute-start.15 = (bf16[256,4096]{1,0:T(8,128)(2,1)S(1)}, bf16[256,4096]{1,0:T(8,128)(2,1)S(1)}, u32[]{:S(2)}, u32[]{:S(2)}) collective-permute-start(bf16[256,4096]{1,0:T(8,128)(2,1)S(1)} %shard_map.84), channel_id=1, source_target_pairs={{0,4},{4,0},{64,68},{68,64},{8,12},{12,8},{72,76},{76,72},{1,5},{5... | collective-permute-start | bytes 6291464 | tf_op jit(solution)/shard_map/ppermute | solution.py:68
  80.6 26.1 %collective-permute-start.16 = (bf16[256,4096]{1,0:T(8,128)(2,1)S(1)}, bf16[256,4096]{1,0:T(8,128)(2,1)S(1)}, u32[]{:S(2)}, u32[]{:S(2)}) collective-permute-start(bf16[256,4096]{1,0:T(8,128)(2,1)S(1)} %shard_map.82), channel_id=1, source_target_pairs={{0,16},{4,52},{64,80},{68,116},{8,24},{12,60},{72,88},{76,124},{1,... | collective-permute-start | bytes 6291464 | tf_op jit(solution)/shard_map/ppermute | solution.py:68
  80.7 28.1 %collective-permute-start.21 = (bf16[512,2048]{1,0:T(8,128)(2,1)S(1)}, bf16[512,2048]{1,0:T(8,128)(2,1)S(1)}, u32[]{:S(2)}, u32[]{:S(2)}) collective-permute-start(bf16[512,2048]{1,0:T(8,128)(2,1)S(1)} %shard_map.80), channel_id=1, source_target_pairs={{0,1},{4,7},{64,65},{68,71},{8,9},{12,15},{72,73},{76,79},{1,0},{5... | collective-permute-start | bytes 6291464 | tf_op jit(solution)/shard_map/ppermute | solution.py:68
  107.5 16.1 %collective-permute-start.17 = (bf16[128,4096]{1,0:T(8,128)(2,1)S(1)}, bf16[128,4096]{1,0:T(8,128)(2,1)S(1)}, u32[]{:S(2)}, u32[]{:S(2)}) collective-permute-start(bf16[128,4096]{1,0:T(8,128)(2,1)S(1)} %slice.28), channel_id=1, source_target_pairs={{0,48},{4,20},{64,112},{68,84},{8,56},{12,28},{72,120},{76,92},{1,... | collective-permute-start | bytes 3145736 | tf_op jit(solution)/shard_map/ppermute | solution.py:68
  108.8 15.0 %copy-start.33 = (bf16[512,2048]{1,0:T(8,128)(2,1)}, bf16[512,2048]{1,0:T(8,128)(2,1)S(1)}, u32[]{:S(2)}) copy-start(bf16[512,2048]{1,0:T(8,128)(2,1)S(1)} %collective-permute-done.21.refs_16_) | copy-start | bytes 6291460
  108.8 29.9 %collective-permute-start.22 = (bf16[512,2048]{1,0:T(8,128)(2,1)}, bf16[512,2048]{1,0:T(8,128)(2,1)}, u32[]{:S(2)}, u32[]{:S(2)}) collective-permute-start(bf16[512,2048]{1,0:T(8,128)(2,1)} %shard_map.83), channel_id=1, source_target_pairs={{0,1},{4,7},{64,65},{68,71},{8,9},{12,15},{72,73},{76,79},{1,0},{5... | collective-permute-start | bytes 6291464 | tf_op jit(solution)/shard_map/ppermute | solution.py:68
  125.3 16.4 %collective-permute-start.18 = (bf16[64,4096]{1,0:T(8,128)(2,1)}, bf16[64,4096]{1,0:T(8,128)(2,1)}, u32[]{:S(2)}, u32[]{:S(2)}) collective-permute-start(bf16[64,4096]{1,0:T(8,128)(2,1)} %slice.29), channel_id=1, source_target_pairs={{0,72},{4,68},{64,0},{68,12},{8,64},{12,76},{72,8},{76,4},{1,73},{... | collective-permute-start | bytes 1572872 | tf_op jit(solution)/shard_map/ppermute | solution.py:68
  135.7 6.1 %copy-start.51 = (f32[128,4096]{1,0:T(8,128)S(1)}, f32[128,4096]{1,0:T(8,128)}, u32[]{:S(2)}) copy-start(f32[128,4096]{1,0:T(8,128)} %copy-done.50) | copy-start | bytes 6291460
  138.6 5.2 %copy-start.28 = (bf16[512,1024]{1,0:T(8,128)(2,1)S(1)}, bf16[512,1024]{1,0:T(8,128)(2,1)}, u32[]{:S(2)}) copy-start(bf16[512,1024]{1,0:T(8,128)(2,1)} %copy-done.27) | copy-start | bytes 3145732
  138.6 16.1 %collective-permute-start.23 = (bf16[512,1024]{1,0:T(8,128)(2,1)S(1)}, bf16[512,1024]{1,0:T(8,128)(2,1)S(1)}, u32[]{:S(2)}, u32[]{:S(2)}) collective-permute-start(bf16[512,1024]{1,0:T(8,128)(2,1)S(1)} %shard_map.87), channel_id=1, source_target_pairs={{0,3},{4,5},{64,67},{68,69},{8,11},{12,13},{72,75},{76,77},{1,2},{... | collective-permute-start | bytes 3145736 | tf_op jit(solution)/shard_map/ppermute | solution.py:68
  142.9 15.8 %collective-permute-start.19 = (bf16[64,4096]{1,0:T(8,128)(2,1)S(1)}, bf16[64,4096]{1,0:T(8,128)(2,1)S(1)}, u32[]{:S(2)}, u32[]{:S(2)}) collective-permute-start(bf16[64,4096]{1,0:T(8,128)(2,1)S(1)} %fusion), channel_id=1, source_target_pairs={{0,8},{4,12},{64,72},{68,76},{8,0},{12,4},{72,64},{76,68},{1,9},{5... | collective-permute-start | bytes 1572872 | tf_op jit(solution)/shard_map/ppermute | solution.py:68
  155.7 17.4 %collective-permute-start.24 = (bf16[512,1024]{1,0:T(8,128)(2,1)}, bf16[512,1024]{1,0:T(8,128)(2,1)}, u32[]{:S(2)}, u32[]{:S(2)}) collective-permute-start(bf16[512,1024]{1,0:T(8,128)(2,1)} %shard_map.86), channel_id=1, source_target_pairs={{0,3},{4,5},{64,67},{68,69},{8,11},{12,13},{72,75},{76,77},{1,2},{... | collective-permute-start | bytes 3145736 | tf_op jit(solution)/shard_map/ppermute | solution.py:68
  159.6 18.9 %collective-permute-start.20 = (bf16[64,4096]{1,0:T(8,128)(2,1)}, bf16[64,4096]{1,0:T(8,128)(2,1)}, u32[]{:S(2)}, u32[]{:S(2)}) collective-permute-start(bf16[64,4096]{1,0:T(8,128)(2,1)} %add_convert_fusion), channel_id=1, source_target_pairs={{0,4},{4,0},{64,68},{68,64},{8,12},{12,8},{72,76},{76,72},{1,5},{5... | collective-permute-start | bytes 1572872 | tf_op jit(solution)/shard_map/ppermute | solution.py:68
  (31 other events, 51.3 us)
